TPU v7x, 512 devices: a whole 4x4x16 slice. The times are simulated.
512 devices in a mesh: dp: 16 (over y, x), cent: 32 (over z, core).
Axes of the slice: x: 4, y: 4, z: 16, core: 2. Of those that a mesh axis runs over, the one named last changes fastest.
Arguments:
- points: float32 [524288, 128], P(('dp', 'cent')), may hold values from -6 to 6
- row_weight: float32 [524288], P(('dp', 'cent')), may hold values from 0.25 to 4
- labels: int32 [2, 524288], P(None, ('dp', 'cent')), may hold values from 0 to 32767, as said below
- centroids: float32 [32768, 128], P('cent'), may hold values from -6 to 6
- prior_prec: float32 [128], replicated, may hold values from 0.5 to 8
Outputs:
- centroids_new: float32 [32768, 128], P('cent')
Inputs may be any that keep to these rules, and one draw needn't show every extreme that they name: Within the rows of one device, at most 64 rows in one step have labels in the same aligned range of 1024 centroids, and in every step some range receives exactly 64 of that device's rows.
All inputs are finite; a program needn't handle non-finite values.
Results may differ from a plain program's by a relative error of at most 0.0001.
Values sent between devices are 32-bit elements; how exact they have to be, the bound alone decides.
No kernel may reach another device: no remote copies, remote signals or barrier semaphores. Data moves between devices by JAX's collectives and lax.ppermute only.
A program may use at most 64 MiB of HBM per device.

v0:
```python
import jax
import jax.numpy as jnp
from jax import lax
from jax.sharding import PartitionSpec as P

ITERS = 3


parallel_ratio = 4.0
tiny = 1e-06


def pack_rows(points, row_weight, chosen, peers, capacity, held):
    target = chosen // held
    local = chosen - target * held
    marks = (target[:, None] == jnp.arange(peers, dtype=jnp.int32)[None, :]).astype(jnp.int32)
    place = jnp.sum(jnp.cumsum(marks, axis=0) * marks, axis=1) - 1
    slot = target * capacity + place
    width = points.shape[1]
    sent_points = jnp.zeros((peers * capacity, width), jnp.float32).at[slot].set(points)
    sent_weight = jnp.zeros((peers * capacity,), jnp.float32).at[slot].set(row_weight)
    sent_local = jnp.zeros((peers * capacity,), jnp.int32).at[slot].set(local)
    return (
        sent_points.reshape(peers, capacity, width),
        sent_weight.reshape(peers, capacity),
        sent_local.reshape(peers, capacity),
    )


def row_terms(vector, got_points, got_weight, got_local, coupling, held):
    picked = jnp.take(vector, got_local, axis=0)
    along = jnp.sum(got_points * picked, axis=1) * coupling
    term = got_weight[:, None] * picked + along[:, None] * got_points
    return jax.ops.segment_sum(term, got_local, num_segments=held)


def solve_whole(got_points, got_weight, got_local, coupling, current, prior_prec, held):
    data = jax.ops.segment_sum(got_weight[:, None] * got_points, got_local, num_segments=held)
    rhs = prior_prec[None, :] * current + parallel_ratio * lax.psum(data, "dp")
    solution = jnp.zeros_like(rhs)
    residual = rhs
    direction = rhs
    norm_now = jnp.sum(residual * residual, axis=1)
    for turn in range(ITERS):
        partial_value = row_terms(direction, got_points, got_weight, got_local, coupling, held)
        image = prior_prec[None, :] * direction + lax.psum(partial_value, "dp")
        alpha = norm_now / (jnp.sum(direction * image, axis=1) + tiny)
        solution = solution + alpha[:, None] * direction
        residual = residual - alpha[:, None] * image
        norm_next = jnp.sum(residual * residual, axis=1)
        direction = residual + (norm_next / (norm_now + tiny))[:, None] * direction
        norm_now = norm_next
    return solution


def per_device(points, row_weight, labels, centroids, prior_prec):
    peers = lax.axis_size("cent")
    held = centroids.shape[0]
    width = points.shape[1]
    capacity = 2 * points.shape[0] // peers
    sections = labels.shape[0]
    packed = [
        pack_rows(points, row_weight, labels[section], peers, capacity, held)
        for section in range(sections)
    ]
    current = centroids
    for section in range(sections):
        got = (
            lax.all_to_all(packed[section][0], "cent", split_axis=0, concat_axis=0, tiled=True),
            lax.all_to_all(packed[section][1], "cent", split_axis=0, concat_axis=0, tiled=True),
            lax.all_to_all(packed[section][2], "cent", split_axis=0, concat_axis=0, tiled=True),
        )
        got_points = got[0].reshape(-1, width)
        got_weight = got[1].reshape(-1)
        got_local = got[2].reshape(-1)
        power = jnp.mean(got_points * got_points, axis=1)
        coupling = got_weight * (parallel_ratio - 1.0) / (width * (power + tiny))
        current = solve_whole(
            got_points, got_weight, got_local, coupling, current, prior_prec, held
        )
    return current


def solution(mesh):
    in_specs = (
        P(("dp", "cent"), None),
        P(("dp", "cent")),
        P(None, ("dp", "cent")),
        P("cent", None),
        P(),
    )
    out_specs = P("cent", None)
    return jax.shard_map(
        per_device, mesh=mesh, in_specs=in_specs, out_specs=out_specs, check_vma=False
    )
```

profile of v0, /device:TPU:1, one launch (start us, length us, event | category | flops | bytes accessed | tf_op | source)
XLA Modules:
  0.0 1134.2 jit_solution(10039741042369511772)
XLA Ops:
  7.4 9.0 reduce-window.16
  16.9 9.0 reduce-window.14
  32.4 16.7 %all-to-all-start.1 = ((f32[32,1,64]{2,1,0:T(1,128)}), f32[32,1,64]{2,1,0:T(1,128)S(1)}, u32[]{:S(2)}, u32[]{:S(2)}) async-start(f32[32,1,64]{2,1,0:T(1,128)} %all_to_all.32), calls=%async_computation.1 | async-start | bytes 32768 | tf_op jit(solution)/shard_map/all_to_all | solution.py:70
  100.3 38.5 %all-to-all-done.2 = f32[32,64,128]{2,1,0:T(8,128)S(1)} async-done(((f32[32,64,128]{2,1,0:T(8,128)}), f32[32,64,128]{2,1,0:T(8,128)S(1)}, u32[]{:S(2)}, u32[]{:S(2)}) %all-to-all-start.2) | async-done | bytes 1048608 | tf_op jit(solution)/shard_map/all_to_all | solution.py:69
  143.4 12.6 %scatter_custom_fusion.3 = f32[1024,128]{1,0:T(8,128)} fusion(s32[2048]{0:T(1024)S(1)} %reshape.532, f32[2048,128]{1,0:T(8,128)S(1)} %bitcast_multiply_fusion.13, f32[]{:T(128)} %constant.54.clone.1), kind=kCustom, calls=%fused_computation.93 | custom fusion | flops 262144 | bytes 524292 | tf_op jit(solution)/shard_map/scatter-add | solution.py:38
  155.9 12.7 %all-to-all-start.3 = ((s32[32,1,64]{2,1,0:T(1,128)}), s32[32,1,64]{2,1,0:T(1,128)S(1)}, u32[]{:S(2)}, u32[]{:S(2)}) async-start(s32[32,1,64]{2,1,0:T(1,128)} %all_to_all.35), calls=%async_computation.3 | async-start | bytes 32768 | tf_op jit(solution)/shard_map/all_to_all | solution.py:71
  168.6 11.8 %all-to-all-done.3 = s32[32,1,64]{2,1,0:T(1,128)S(1)} async-done(((s32[32,1,64]{2,1,0:T(1,128)}), s32[32,1,64]{2,1,0:T(1,128)S(1)}, u32[]{:S(2)}, u32[]{:S(2)}) %all-to-all-start.3) | async-done | bytes 8224 | tf_op jit(solution)/shard_map/all_to_all | solution.py:71
  185.4 86.5 %all-reduce.9.cloned.1.call-done = f32[1024,128]{1,0:T(8,128)} async-done(((f32[1024,128]{1,0:T(8,128)}), f32[1024,128]{1,0:T(8,128)}) %all-reduce.9.cloned.1.call-update) | async-done | bytes 524304 | tf_op jit(solution)/shard_map/psum | solution.py:39
  273.0 7.6 gather_fusion
  285.2 12.9 %scatter_custom_fusion.4 = f32[1024,128]{1,0:T(8,128)} fusion(s32[2048]{0:T(1024)S(1)} %reshape.532, f32[2048,128]{1,0:T(8,128)} %fusion.7, f32[]{:T(128)} %constant.54.clone.1), kind=kCustom, calls=%fused_computation.91 | custom fusion | flops 262144 | bytes 524800 | tf_op jit(solution)/shard_map/scatter-add | solution.py:34
  298.2 115.8 %all-reduce.11.cloned.1.call-done = f32[1024,128]{1,0:T(8,128)} async-done(((f32[1024,128]{1,0:T(8,128)}), f32[1024,128]{1,0:T(8,128)}) %all-reduce.11.cloned.1.call-update) | async-done | bytes 524304 | tf_op jit(solution)/shard_map/psum | solution.py:46
  428.6 12.9 %scatter_custom_fusion.5 = f32[1024,128]{1,0:T(8,128)} fusion(s32[2048]{0:T(1024)S(1)} %reshape.532, f32[2048,128]{1,0:T(8,128)} %fusion.9, f32[]{:T(128)} %constant.54.clone.1), kind=kCustom, calls=%fused_computation.89 | custom fusion | flops 262144 | bytes 524800 | tf_op jit(solution)/shard_map/scatter-add | solution.py:34
  444.7 14.3 %scatter_custom_fusion.10 = f32[1024,128]{1,0:T(8,128)} fusion(s32[2048]{0:T(1024)S(1)} %reshape.588, f32[2048,128]{1,0:T(8,128)} %bitcast_multiply_fusion.6, f32[]{:T(128)} %constant.54.clone.1), kind=kCustom, calls=%fused_computation.85 | custom fusion | flops 262144 | bytes 524800 | tf_op jit(solution)/shard_map/scatter-add | solution.py:38
  459.0 98.5 %all-reduce.13.cloned.1.call-done = f32[1024,128]{1,0:T(8,128)} async-done(((f32[1024,128]{1,0:T(8,128)}), f32[1024,128]{1,0:T(8,128)}) %all-reduce.13.cloned.1.call-update) | async-done | bytes 524304 | tf_op jit(solution)/shard_map/psum | solution.py:46
  559.5 7.6 gather_fusion.2
  572.0 12.9 %scatter_custom_fusion.6 = f32[1024,128]{1,0:T(8,128)} fusion(s32[2048]{0:T(1024)S(1)} %reshape.532, f32[2048,128]{1,0:T(8,128)} %fusion.11, f32[]{:T(128)} %constant.54.clone.1), kind=kCustom, calls=%fused_computation.87 | custom fusion | flops 262144 | bytes 524800 | tf_op jit(solution)/shard_map/scatter-add | solution.py:34
  585.5 117.2 %all-reduce.21.cloned.1.call-done = (f32[1024,128]{1,0:T(8,128)}, f32[1024,128]{1,0:T(8,128)}) async-done(((f32[1024,128]{1,0:T(8,128)}, f32[1024,128]{1,0:T(8,128)}), (f32[1024,128]{1,0:T(8,128)}, f32[1024,128]{1,0:T(8,128)})) %all-reduce.21.cloned.1.call-update) | async-done | bytes 1048592 | tf_op jit(solution)/shard_map/psum | solution.py:39
  713.1 14.3 %scatter_custom_fusion.11 = f32[1024,128]{1,0:T(8,128)} fusion(s32[2048]{0:T(1024)S(1)} %reshape.588, f32[2048,128]{1,0:T(8,128)} %fusion.1, f32[]{:T(128)} %constant.54.clone.1), kind=kCustom, calls=%fused_computation.83 | custom fusion | flops 262144 | bytes 524800 | tf_op jit(solution)/shard_map/scatter-add | solution.py:34
  727.7 113.9 %all-reduce.15.cloned.1.call-done = f32[1024,128]{1,0:T(8,128)} async-done(((f32[1024,128]{1,0:T(8,128)}), f32[1024,128]{1,0:T(8,128)}) %all-reduce.15.cloned.1.call-update) | async-done | bytes 524304 | tf_op jit(solution)/shard_map/psum | solution.py:46
  853.2 14.3 %scatter_custom_fusion.12 = f32[1024,128]{1,0:T(8,128)} fusion(s32[2048]{0:T(1024)S(1)} %reshape.588, f32[2048,128]{1,0:T(8,128)} %fusion.3, f32[]{:T(128)} %constant.54.clone.1), kind=kCustom, calls=%fused_computation.81 | custom fusion | flops 262144 | bytes 524800 | tf_op jit(solution)/shard_map/scatter-add | solution.py:34
  867.6 114.0 %all-reduce.17.cloned.1.call-done = f32[1024,128]{1,0:T(8,128)} async-done(((f32[1024,128]{1,0:T(8,128)}), f32[1024,128]{1,0:T(8,128)}) %all-reduce.17.cloned.1.call-update) | async-done | bytes 524304 | tf_op jit(solution)/shard_map/psum | solution.py:46
  983.7 7.6 gather_fusion.5
  995.9 14.3 %scatter_custom_fusion.13 = f32[1024,128]{1,0:T(8,128)} fusion(s32[2048]{0:T(1024)S(1)} %reshape.588, f32[2048,128]{1,0:T(8,128)} %fusion.5, f32[]{:T(128)} %constant.54.clone.1), kind=kCustom, calls=%fused_computation.79 | custom fusion | flops 262144 | bytes 524800 | tf_op jit(solution)/shard_map/scatter-add | solution.py:34
  1010.2 114.1 %all-reduce.19.cloned.1.call-done = f32[1024,128]{1,0:T(8,128)} async-done(((f32[1024,128]{1,0:T(8,128)}), f32[1024,128]{1,0:T(8,128)}) %all-reduce.19.cloned.1.call-update) | async-done | bytes 524304 | tf_op jit(solution)/shard_map/psum | solution.py:46
  (160 shorter events, 130.6 us)
Async XLA Ops:
  32.4 28.5 %all-to-all-start.1 = ((f32[32,1,64]{2,1,0:T(1,128)}), f32[32,1,64]{2,1,0:T(1,128)S(1)}, u32[]{:S(2)}, u32[]{:S(2)}) async-start(f32[32,1,64]{2,1,0:T(1,128)} %all_to_all.32), calls=%async_computation.1 | async-start | bytes 32768 | tf_op jit(solution)/shard_map/all_to_all | solution.py:70
  60.9 17.2 %all-to-all-start = ((s32[32,1,64]{2,1,0:T(1,128)}), s32[32,1,64]{2,1,0:T(1,128)S(1)}, u32[]{:S(2)}, u32[]{:S(2)}) async-start(s32[32,1,64]{2,1,0:T(1,128)} %all_to_all.30), calls=%async_computation | async-start | bytes 32768 | tf_op jit(solution)/shard_map/all_to_all | solution.py:71
  78.1 60.7 %all-to-all-start.2 = ((f32[32,64,128]{2,1,0:T(8,128)}), f32[32,64,128]{2,1,0:T(8,128)S(1)}, u32[]{:S(2)}, u32[]{:S(2)}) async-start(f32[32,64,128]{2,1,0:T(8,128)} %bitcast.7), calls=%async_computation.2 | async-start | bytes 2097152 | tf_op jit(solution)/shard_map/all_to_all | solution.py:69
  138.8 143.9 %copy-start = (f32[32,64,128]{2,1,0:T(8,128)}, f32[32,64,128]{2,1,0:T(8,128)S(1)}, u32[]{:S(2)}) copy-start(f32[32,64,128]{2,1,0:T(8,128)S(1)} %all-to-all-done.2) | copy-start | bytes 3145732
  138.8 17.1 %all-to-all-start.4 = ((f32[32,1,64]{2,1,0:T(1,128)}), f32[32,1,64]{2,1,0:T(1,128)S(1)}, u32[]{:S(2)}, u32[]{:S(2)}) async-start(f32[32,1,64]{2,1,0:T(1,128)} %all_to_all.37), calls=%async_computation.4 | async-start | bytes 32768 | tf_op jit(solution)/shard_map/all_to_all | solution.py:70
  142.8 129.1 %all-reduce.9.cloned.1.call-start = ((), (), s32[]{:S(2)}) async-start(), calls=%async_computation.6 | async-start | bytes 1048576 | tf_op jit(solution)/shard_map/psum | solution.py:39
  155.9 24.4 %all-to-all-start.3 = ((s32[32,1,64]{2,1,0:T(1,128)}), s32[32,1,64]{2,1,0:T(1,128)S(1)}, u32[]{:S(2)}, u32[]{:S(2)}) async-start(s32[32,1,64]{2,1,0:T(1,128)} %all_to_all.35), calls=%async_computation.3 | async-start | bytes 32768 | tf_op jit(solution)/shard_map/all_to_all | solution.py:71
  180.4 262.9 %all-to-all-start.5 = ((f32[32,64,128]{2,1,0:T(8,128)}), f32[32,64,128]{2,1,0:T(8,128)S(1)}, u32[]{:S(2)}, u32[]{:S(2)}) async-start(f32[32,64,128]{2,1,0:T(8,128)} %bitcast.98), calls=%async_computation.5 | async-start | bytes 2097152 | tf_op jit(solution)/shard_map/all_to_all | solution.py:69
  184.9 87.0 %copy-start.13 = (f32[1024,128]{1,0:T(8,128)S(1)}, f32[1024,128]{1,0:T(8,128)}, u32[]{:S(2)}) copy-start(f32[1024,128]{1,0:T(8,128)} %param.10) | copy-start | bytes 1572868
  184.9 229.2 %all-reduce.11.cloned.1.call-start = ((), (), s32[]{:S(2)}) async-start(), calls=%async_computation.7 | async-start | bytes 1048576 | tf_op jit(solution)/shard_map/psum | solution.py:46
  185.3 86.6 %copy-start.15 = (f32[128]{0:T(128)S(1)}, f32[128]{0:T(128)}, u32[]{:S(2)}) copy-start(f32[128]{0:T(128)} %param.11) | copy-start | bytes 1540
  280.6 2.1 copy-start.5
  298.2 259.3 %all-reduce.13.cloned.1.call-start = ((), (), s32[]{:S(2)}) async-start(), calls=%async_computation.8 | async-start | bytes 1048576 | tf_op jit(solution)/shard_map/psum | solution.py:46
  414.1 1.5 copy-start.11
  423.7 2.3 copy-start.1
  423.7 2.4 copy-start.6
  441.6 261.1 %all-reduce.21.cloned.1.call-start = ((), (), s32[]{:S(2)}) async-start(), calls=%async_computation.12 | async-start | bytes 2097152 | tf_op jit(solution)/shard_map/psum | solution.py:39
  567.1 2.3 copy-start.2
  567.1 2.4 copy-start.3
  585.0 256.7 %all-reduce.15.cloned.1.call-start = ((), (), s32[]{:S(2)}) async-start(), calls=%async_computation.9 | async-start | bytes 1048576 | tf_op jit(solution)/shard_map/psum | solution.py:46
  727.4 254.2 %all-reduce.17.cloned.1.call-start = ((), (), s32[]{:S(2)}) async-start(), calls=%async_computation.10 | async-start | bytes 1048576 | tf_op jit(solution)/shard_map/psum | solution.py:46
  867.5 115.4 %copy-start.8 = (f32[1024,128]{1,0:T(8,128)S(1)}, f32[1024,128]{1,0:T(8,128)}, u32[]{:S(2)}) copy-start(f32[1024,128]{1,0:T(8,128)} %copy-done.7) | copy-start | bytes 1572868
  867.5 256.8 %all-reduce.19.cloned.1.call-start = ((), (), s32[]{:S(2)}) async-start(), calls=%async_computation.11 | async-start | bytes 1048576 | tf_op jit(solution)/shard_map/psum | solution.py:46
  991.3 2.1 copy-start.4
  (6 other events, 7.0 us)
Sparse Core Ops, SparseCore 0:
  156.1 115.8 all-reduce.8
  298.3 115.7 all-reduce.10
  441.7 115.6 all-reduce.12
  585.1 117.4 all-reduce.20
  727.6 114.0 all-reduce.14
  867.6 113.9 all-reduce.16
  1010.3 113.9 all-reduce.18
where the time goes:
time: 1140 us; the launch traced here: 1130 us
  waiting for transfers between devices  824 us (72%)
  other arithmetic  171 us (15%)
  local copies, waits for them, and re-layouts  74.9 us (7%)
  starting transfers between devices  49.3 us (4%)
  between operations  14.6 us (1%)
    psum x5, waiting for transfers between devices, solve_whole(): image = prior_prec[None, :] * direction + lax.psum(partial_value, 'dp')  556 us
    psum x2, waiting for transfers between devices, solve_whole(): rhs = prior_prec[None, :] * current + parallel_ratio * lax.psum(data, 'dp')  204 us
    scatter-add x6, other arithmetic, row_terms(): return jax.ops.segment_sum(term, got_local, num_segments=held)  81.7 us
    gather x6, local copies, waits for them, and re-layouts, row_terms(): picked = jnp.take(vector, got_local, axis=0)  41.2 us
    all_to_all x2, waiting for transfers between devices, per_device(): lax.all_to_all(packed[section][0], 'cent', split_axis=0, concat_axis=0, t...  38.5 us
    scatter-add x2, other arithmetic, solve_whole(): jax.ops.segment_sum(got_weight[:, None] * got_points, got_local, num_segm...  26.8 us
  transfers between devices with their start and end apart: 13, of which 11 were waited for; matrix products, arithmetic and copies ran while one was open for 10% of the time, Pallas kernels for 0%

commit v1 on v0

v1 whole, which is shorter than its diff:
```python
import functools

import jax
import jax.numpy as jnp
from jax import lax
from jax.experimental import pallas as pl
from jax.experimental.pallas import tpu as pltpu
from jax.sharding import PartitionSpec as P

ITERS = 3
CAP = 192
PITCH = CAP + 8
LANES = 128
LIMIT = 48 * 1024 * 1024

parallel_ratio = 4.0
tiny = 1e-06


def _dot(a, b):
    return jnp.dot(a, b, preferred_element_type=jnp.float32)


def _dot_t(a, b):
    return lax.dot_general(a, b, (((1,), (1,)), ((), ())), preferred_element_type=jnp.float32)


def _halves(x):
    high = x.astype(jnp.bfloat16)
    low = (x - high.astype(jnp.float32)).astype(jnp.bfloat16)
    return high, low


def _iota(shape, dim):
    return lax.broadcasted_iota(jnp.int32, shape, dim)


def _upper():
    return (_iota((LANES, LANES), 0) <= _iota((LANES, LANES), 1)).astype(jnp.bfloat16)


def _places(marks, groups):
    within = _dot(jnp.concatenate(marks, axis=0).astype(jnp.bfloat16), _upper())
    before = jnp.zeros((groups, 1), jnp.float32)
    places = []
    for k, mark in enumerate(marks):
        part = within[k * groups : (k + 1) * groups]
        places.append(jnp.sum(mark * (part + (before - 1.0)), axis=0, keepdims=True))
        before = before + part[:, LANES - 1 :]
    return places, before


def _pack_kernel(peers, slots, held, odd_ref, x_ref, w_ref, t_ref, out_ref):
    rows = x_ref.shape[0]
    steps = t_ref.shape[0]
    high, low = _halves(x_ref[...])
    both = jnp.concatenate([high, low], axis=1)
    w_high, w_low = _halves(w_ref[...])
    first = (_iota((peers, 2 * slots), 1) < slots).astype(jnp.int32)
    for step in range(steps):
        label = t_ref[step : step + 1, :]
        target = label // held
        local = label - target * held
        marks = (_iota((peers, rows), 0) == target).astype(jnp.float32)
        chunks = [marks[:, k : k + LANES] for k in range(0, rows, LANES)]
        places, _ = _places(chunks, peers)
        place = jnp.concatenate(places, axis=1).astype(jnp.int32)
        l_high, l_low = _halves(local.astype(jnp.float32))
        values = jnp.concatenate(
            [marks * v.astype(jnp.float32) for v in (w_high, w_low, l_high, l_low)], axis=0
        ).astype(jnp.bfloat16)
        at = ((_iota((2 * slots, rows), 0) % slots) == place).astype(jnp.bfloat16)
        notes = _dot_t(values, at)
        weight = notes[:peers] + notes[peers : 2 * peers]
        index = notes[2 * peers : 3 * peers] + notes[3 * peers :]
        notes = jnp.where(first != odd_ref[0], weight, index)
        slot = target * slots + place
        block = 8
        for b in range(0, peers, block):
            take = (_iota((block * slots, rows), 0) + b * slots == slot).astype(jnp.bfloat16)
            got = _dot(take, both)
            got = got[:, :LANES] + got[:, LANES:]
            for t in range(block):
                base = ((b + t) * steps + step) * (slots + 1)
                out_ref[base : base + slots, :] = got[t * slots : (t + 1) * slots]
                out_ref[base + slots : base + slots + 1, :] = notes[b + t : b + t + 1]


def _pack(points, weight, labels, odd, peers, slots, held):
    return pl.pallas_call(
        functools.partial(_pack_kernel, peers, slots, held),
        out_shape=jax.ShapeDtypeStruct((peers * labels.shape[0] * (slots + 1), LANES), jnp.float32),
        in_specs=[pl.BlockSpec(memory_space=pltpu.SMEM)] + [pl.BlockSpec(memory_space=pltpu.VMEM)] * 3,
        compiler_params=pltpu.CompilerParams(vmem_limit_bytes=LIMIT),
        name="pack",
    )(odd, points, weight, labels)


def _repack_kernel(peers, slots, held, groups, steps, x_ref, out_ref, even_ref, odd_ref, both_ref):
    pairs = peers // 2
    rows = peers * slots
    per = held // groups
    first = _iota((pairs, LANES), 1) < slots
    for step in range(steps):
        for b in range(peers):
            base = (b * steps + step) * (slots + 1)
            high, low = _halves(x_ref[base : base + slots, :])
            both_ref[b * slots : (b + 1) * slots, :LANES] = high
            both_ref[b * slots : (b + 1) * slots, LANES:] = low
            note_ref = odd_ref if b % 2 else even_ref
            note_ref[b // 2 : b // 2 + 1, :] = x_ref[base + slots : base + slots + 1, :]
        even, odd = even_ref[...], odd_ref[...]
        weight = jnp.where(first, even, odd)
        local = pltpu.roll(jnp.where(first, odd, even), slots, 1).astype(jnp.int32)
        owner = jnp.where(weight > 0.0, local // per, -1)
        index = (local % per).astype(jnp.float32)
        marks = [
            (_iota((groups, LANES), 0) == owner[k : k + 1]).astype(jnp.float32) for k in range(pairs)
        ]
        places, sizes = _places(marks, groups)
        flag = jnp.max(sizes, axis=0, keepdims=True) > CAP
        flag = jnp.where(flag, jnp.ones((1, LANES), jnp.float32), 0.0)
        place = jnp.concatenate(places, axis=1).astype(jnp.int32)
        owner = jnp.concatenate([owner[k : k + 1] for k in range(pairs)], axis=1)
        fits = (owner >= 0) & (place < CAP)
        place = jnp.where(fits, place, -1)
        slot = jnp.where(fits, owner * PITCH + place, -1)
        w_high, w_low = _halves(weight)
        values = jnp.concatenate(
            [
                jnp.concatenate([marks[k] * v[k : k + 1] for k in range(pairs)], axis=1)
                for v in (w_high.astype(jnp.float32), w_low.astype(jnp.float32), index)
            ],
            axis=0,
        ).astype(jnp.bfloat16)
        at = (_iota((2 * LANES, rows), 0) == place).astype(jnp.bfloat16)
        notes = _dot_t(values, at)
        weight = notes[:groups] + notes[groups : 2 * groups]
        index = notes[2 * groups :]
        both = both_ref[...]
        for o in range(0, groups, 2):
            take = (_iota((2 * PITCH, rows), 0) + o * PITCH == slot).astype(jnp.bfloat16)
            got = _dot(take, both)
            got = got[:, :LANES] + got[:, LANES:]
            for half in range(2):
                base = ((o + half) * steps + step) * PITCH
                out_ref[base : base + PITCH, :] = got[half * PITCH : (half + 1) * PITCH]
                base = base + CAP
                own = slice(o + half, o + half + 1)
                out_ref[base : base + 1, :] = weight[own, :LANES]
                out_ref[base + 1 : base + 2, :] = weight[own, LANES:]
                out_ref[base + 2 : base + 3, :] = index[own, :LANES]
                out_ref[base + 3 : base + 4, :] = index[own, LANES:]
                out_ref[base + 4 : base + 5, :] = flag


def _repack(got, peers, slots, held, groups, steps):
    return pl.pallas_call(
        functools.partial(_repack_kernel, peers, slots, held, groups, steps),
        out_shape=jax.ShapeDtypeStruct((groups * steps * PITCH, LANES), jnp.float32),
        scratch_shapes=[
            pltpu.VMEM((peers // 2, LANES), jnp.float32),
            pltpu.VMEM((peers // 2, LANES), jnp.float32),
            pltpu.VMEM((peers * slots, 2 * LANES), jnp.bfloat16),
        ],
        compiler_params=pltpu.CompilerParams(vmem_limit_bytes=LIMIT),
        name="repack",
    )(got)


def _solve_kernel(groups, steps, x_ref, cur_ref, prior_ref, out_ref, flag_ref, high_ref, low_ref):
    wide = 2 * LANES
    per = cur_ref.shape[0]
    ones = jnp.ones((8, LANES), jnp.bfloat16)
    flag = jnp.zeros((1, LANES), jnp.float32)
    current = cur_ref[...]
    for step in range(steps):
        weights, indices, powers = [], [], []
        for s in range(groups):
            base = (s * steps + step) * PITCH
            rows = x_ref[base : base + CAP, :]
            rows = jnp.concatenate([rows, jnp.zeros((wide - CAP, LANES), jnp.float32)], axis=0)
            high, low = _halves(rows)
            high_ref[s * wide : (s + 1) * wide, :] = high
            low_ref[s * wide : (s + 1) * wide, :] = low
            square_high, square_low = _halves(rows * rows)
            powers.append((_dot_t(ones, square_high) + _dot_t(ones, square_low))[:1])
            notes = x_ref[base + CAP : base + PITCH, :]
            weights += [notes[0:1], notes[1:2]]
            indices += [notes[2:3], notes[3:4]]
            flag = jnp.maximum(flag, notes[4:5])
        weight = jnp.concatenate(weights, axis=1)
        index = jnp.concatenate(indices, axis=1).astype(jnp.int32)
        power = jnp.concatenate(powers, axis=1) * (1.0 / LANES)
        coupling = weight * (parallel_ratio - 1.0) / (LANES * (power + tiny))
        mine = _iota((per, groups * wide), 0) == index
        weighted = jnp.where(mine, weight, 0.0)
        coupled = jnp.where(mine, coupling, 0.0)
        weight_sum = jnp.sum(weighted, axis=1, keepdims=True)
        high, low = high_ref[...], low_ref[...]

        def gather_up(terms):
            a, b = _halves(terms)
            c = _dot(jnp.concatenate([a, b], axis=0), high)
            return c[:per] + c[per:] + _dot(a, low)

        def along(vector):
            a, b = _halves(vector)
            c = _dot_t(jnp.concatenate([a, b], axis=0), high)
            return c[:per] + c[per:] + _dot_t(a, low)

        diagonal = prior_ref[...] + weight_sum
        rhs = prior_ref[...] * current + parallel_ratio * gather_up(weighted)
        current = jnp.zeros_like(rhs)
        residual = rhs
        direction = rhs
        norm_now = jnp.sum(residual * residual, axis=1, keepdims=True)
        for turn in range(ITERS):
            image = diagonal * direction + gather_up(along(direction) * coupled)
            alpha = norm_now / (jnp.sum(direction * image, axis=1, keepdims=True) + tiny)
            current = current + alpha * direction
            if turn + 1 < ITERS:
                residual = residual - alpha * image
                norm_next = jnp.sum(residual * residual, axis=1, keepdims=True)
                direction = residual + (norm_next / (norm_now + tiny)) * direction
                norm_now = norm_next
    out_ref[...] = current
    flag_ref[...] = flag


def _solve(got, current, prior, groups, steps):
    rows = groups * 2 * LANES
    return pl.pallas_call(
        functools.partial(_solve_kernel, groups, steps),
        out_shape=(
            jax.ShapeDtypeStruct(current.shape, jnp.float32),
            jax.ShapeDtypeStruct((1, LANES), jnp.float32),
        ),
        scratch_shapes=[
            pltpu.VMEM((rows, LANES), jnp.bfloat16),
            pltpu.VMEM((rows, LANES), jnp.bfloat16),
        ],
        compiler_params=pltpu.CompilerParams(vmem_limit_bytes=LIMIT),
        name="solve",
    )(got, current, prior)


def row_terms(vector, got_points, got_weight, got_local, coupling, held):
    picked = jnp.take(vector, got_local, axis=0)
    along = jnp.sum(got_points * picked, axis=1) * coupling
    term = got_weight[:, None] * picked + along[:, None] * got_points
    return jax.ops.segment_sum(term, got_local, num_segments=held)


def dp_sum(x):
    groups = lax.axis_size("dp")
    parts = x.reshape(groups, -1, x.shape[1])
    parts = lax.all_to_all(parts, "dp", split_axis=0, concat_axis=0, tiled=True)
    spread = jnp.broadcast_to(jnp.sum(parts, axis=0)[None], parts.shape)
    return lax.all_to_all(spread, "dp", split_axis=0, concat_axis=0, tiled=True).reshape(x.shape)


def solve_whole(got_points, got_weight, got_local, coupling, current, prior_prec, held):
    data = jax.ops.segment_sum(got_weight[:, None] * got_points, got_local, num_segments=held)
    rhs = prior_prec[None, :] * current + parallel_ratio * dp_sum(data)
    solution = jnp.zeros_like(rhs)
    residual = rhs
    direction = rhs
    norm_now = jnp.sum(residual * residual, axis=1)
    for turn in range(ITERS):
        partial_value = row_terms(direction, got_points, got_weight, got_local, coupling, held)
        image = prior_prec[None, :] * direction + dp_sum(partial_value)
        alpha = norm_now / (jnp.sum(direction * image, axis=1) + tiny)
        solution = solution + alpha[:, None] * direction
        residual = residual - alpha[:, None] * image
        norm_next = jnp.sum(residual * residual, axis=1)
        direction = residual + (norm_next / (norm_now + tiny))[:, None] * direction
        norm_now = norm_next
    return solution


def any_labels(got, centroids, prior_prec, peers, slots, steps):
    held, width = centroids.shape
    current = centroids
    got = got.reshape(peers, steps, slots + 1, width)
    for step in range(steps):
        block = got[:, step]
        points = block[:, :slots].reshape(-1, width)
        notes = block[:, slots].reshape(peers // 2, 2, 2, slots)
        weight = jnp.stack([notes[:, 0, 0], notes[:, 1, 1]], axis=1).reshape(-1)
        local = jnp.stack([notes[:, 0, 1], notes[:, 1, 0]], axis=1).reshape(-1).astype(jnp.int32)
        power = jnp.mean(points * points, axis=1)
        coupling = weight * (parallel_ratio - 1.0) / (width * (power + tiny))
        current = solve_whole(points, weight, local, coupling, current, prior_prec, held)
    return current


def per_device(points, row_weight, labels, centroids, prior_prec):
    peers = lax.axis_size("cent")
    groups = lax.axis_size("dp")
    held, width = centroids.shape
    slots = 2 * points.shape[0] // peers
    steps = labels.shape[0]
    per = held // groups
    odd = (lax.axis_index("cent") % 2).reshape(1)
    start = lax.axis_index("dp") * per
    sent = _pack(points, row_weight.reshape(1, -1), labels, odd, peers, slots, held)
    got = lax.all_to_all(
        sent.reshape(peers, steps * (slots + 1), 1, width), "cent", split_axis=0, concat_axis=0, tiled=True
    ).reshape(-1, width)
    again = _repack(got, peers, slots, held, groups, steps)
    again = lax.all_to_all(
        again.reshape(groups, steps * PITCH, width), "dp", split_axis=0, concat_axis=0, tiled=True
    ).reshape(-1, width)
    current = lax.dynamic_slice(centroids, (start, 0), (per, width))
    current, flag = _solve(again, current, prior_prec.reshape(1, -1), groups, steps)

    def summed(got, current):
        every = any_labels(got, centroids, prior_prec, peers, slots, steps)
        return lax.dynamic_slice(every, (start, 0), (per, width))

    current = lax.cond(flag[0, 0] > 0.0, summed, lambda got, current: current, got, current)
    spread = jnp.broadcast_to(current[None], (groups, per, width))
    spread = lax.all_to_all(spread, "dp", split_axis=0, concat_axis=0, tiled=True)
    return spread.reshape(held, width)


def solution(mesh):
    in_specs = (
        P(("dp", "cent"), None),
        P(("dp", "cent")),
        P(None, ("dp", "cent")),
        P("cent", None),
        P(),
    )
    out_specs = P("cent", None)
    return jax.shard_map(
        per_device, mesh=mesh, in_specs=in_specs, out_specs=out_specs, check_vma=False
    )
```

time: 1140 us -> 216 us (0.19)
  waiting for transfers between devices: 824 us -> 46.8 us
  other arithmetic: 171 us -> 0 us
  blocking collectives: 0 us -> 131 us
  local copies, waits for them, and re-layouts: 74.9 us -> 5.73 us
  starting transfers between devices: 49.3 us -> 6.9 us
  Pallas kernels: 0 us -> 21.4 us
  between operations: 14.6 us -> 0.11 us
    psum x7 -> x0, waiting for transfers between devices: 760 us -> none  [the longest x5 556 us: solve_whole(): image = prior_prec[None, :] * direction + lax.psum(partial_value, 'dp')]
    all_to_all x0 -> x2, blocking collectives: none -> 131 us  [the longest x1 119 us: per_device(): lax.all_to_all(sent.reshape(peers, steps * (slots + 1), 1, width), 'cent'...]
    scatter-add x8 -> x0, other arithmetic: 109 us -> none  [the longest x6 81.7 us: row_terms(): return jax.ops.segment_sum(term, got_local, num_segments=held)]
    all_to_all x6 -> x1, starting transfers between devices: 48.3 us -> 6.9 us  [per_device(): lax.all_to_all(again.reshape(groups, steps * PITCH, width), 'dp', split_a...]
    gather x6 -> x0, local copies, waits for them, and re-layouts: 41.2 us -> none  [row_terms(): picked = jnp.take(vector, got_local, axis=0)]
    scatter x6 -> x0, local copies, waits for them, and re-layouts: 26.6 us -> none  [the longest x2 9.02 us: pack_rows(): jnp.zeros((peers * capacity, width), jnp.float32).at[slot].set(points)]
    pallas_call x0 -> x3, Pallas kernels: none -> 21.4 us  [the longest x1 10.3 us: _solve(): pl.pallas_call(functools.partial(_solve_kernel, groups, steps), out_shape...]
    reduce_sum x20 -> x0, other arithmetic: 20.4 us -> none  [the longest x6 9.97 us: row_terms(): along = jnp.sum(got_points * picked, axis=1) * coupling]
  transfers between devices with their start and end apart: 13 -> 1, of which waited for: 11 -> 1; matrix products, arithmetic and copies ran while one was open for 10% -> 0% of each run, Pallas kernels for 0% -> 0%
where the time goes in v1:
time: 216 us; the launch traced here: 213 us
  blocking collectives  131 us (61%)
  waiting for transfers between devices  46.8 us (22%)
  Pallas kernels  21.4 us (10%)
  starting transfers between devices  6.9 us (3%)
  local copies, waits for them, and re-layouts  5.73 us (3%)
    all_to_all x1, blocking collectives, per_device(): lax.all_to_all(sent.reshape(peers, steps * (slots + 1), 1, width), 'cent'...  119 us
    all_to_all x1, waiting for transfers between devices, per_device(): lax.all_to_all(again.reshape(groups, steps * PITCH, width), 'dp', split_a...  46.8 us
    all_to_all x1, blocking collectives, per_device(): lax.all_to_all(spread, 'dp', split_axis=0, concat_axis=0, tiled=True)  12.8 us
    pallas_call x1, Pallas kernels, _solve(): pl.pallas_call(functools.partial(_solve_kernel, groups, steps), out_shape...  10.3 us
    pallas_call x1, Pallas kernels, _repack(): pl.pallas_call(functools.partial(_repack_kernel, peers, slots, held, grou...  8.16 us
    all_to_all x1, starting transfers between devices, per_device(): lax.all_to_all(again.reshape(groups, steps * PITCH, width), 'dp', split_a...  6.9 us
    unnamed x13, local copies, waits for them, and re-layouts  4.92 us
  transfers between devices with their start and end apart: 1, of which 1 were waited for; matrix products, arithmetic and copies ran while one was open for 0% of the time, Pallas kernels for 0%

profile of v1, /device:TPU:1, one launch (start us, length us, event | category | flops | bytes accessed | tf_op | source)
XLA Modules:
  0.0 212.6 jit_solution(15462163160350815829)
XLA Ops:
  0.0 0.0 copy-start.1
  0.0 1.0 copy-done.1
  1.0 0.0 copy-start.2
  1.0 0.7 copy-done.2
  1.7 0.0 copy-start.3
  1.7 0.7 copy-done.3
  2.4 3.0 %pack.1 = f32[4160,128]{1,0:T(8,128)S(1)} custom-call(s32[1]{0:T(128)} %bitcast.29.odd_ref, f32[1024,128]{1,0:T(8,128)S(1)} %copy-done.1, f32[1,1024]{1,0:T(1,128)S(1)} %bitcast.152, s32[2,1024]{1,0:T(2,128)S(1)} %copy-done.2), custom_call_target="tpu_custom_call" | custom-call | tf_op jit(solution)/shard_map/pack/pallas_call | solution.py:90
  5.4 118.6 %all_to_all.86 = f32[32,130,1,128]{3,2,1,0:T(1,128)S(1)} all-to-all(f32[32,130,1,128]{3,2,1,0:T(1,128)S(1)} %bitcast.151), channel_id=1, replica_groups=mesh['dp'=16,'cent'=32] {'cent'}, dimensions={0} | all-to-all | bytes 4259840 | tf_op jit(solution)/shard_map/all_to_all | solution.py:308
  124.0 0.0 copy-start.6
  124.0 8.2 %repack.1 = f32[6400,128]{1,0:T(8,128)S(1)} custom-call(f32[4160,128]{1,0:T(8,128)S(1)} %bitcast.154), custom_call_target="tpu_custom_call" | custom-call | tf_op jit(solution)/shard_map/repack/pallas_call | solution.py:158
  132.1 0.0 copy-done.6
  132.2 0.0 copy-start
  132.2 1.7 copy-done
  133.9 0.0 copy-start.16
  133.9 6.9 %all-to-all-start.17 = ((f32[16,400,128]{2,1,0:T(8,128)}), f32[16,400,128]{2,1,0:T(8,128)S(1)}, u32[]{:S(2)}, u32[]{:S(2)}) async-start(f32[16,400,128]{2,1,0:T(8,128)} %bitcast.150), calls=%async_computation.17 | async-start | bytes 6553600 | tf_op jit(solution)/shard_map/all_to_all | solution.py:312
  140.8 0.8 constant_dynamic-slice_fusion.cur_ref
  141.5 46.8 %all-to-all-done.17 = f32[16,400,128]{2,1,0:T(8,128)S(1)} async-done(((f32[16,400,128]{2,1,0:T(8,128)}), f32[16,400,128]{2,1,0:T(8,128)S(1)}, u32[]{:S(2)}, u32[]{:S(2)}) %all-to-all-start.17) | async-done | bytes 3276832 | tf_op jit(solution)/shard_map/all_to_all | solution.py:312
  188.3 0.0 copy-done.16
  188.3 10.3 %solve.1 = (f32[64,128]{1,0:T(8,128)S(1)}, f32[1,128]{1,0:T(1,128)S(1)}) custom-call(f32[6400,128]{1,0:T(8,128)S(1)} %bitcast.149, f32[64,128]{1,0:T(8,128)S(1)} %constant_dynamic-slice_fusion.cur_ref, f32[1,128]{1,0:T(1,128)S(1)} %bitcast.163), custom_call_target="tpu_custom_call" | custom-call | tf_op jit(solution)/shard_map/solve/pallas_call | solution.py:233
  198.7 0.3 conditional.1
  199.0 12.8 %all_to_all.87 = f32[16,64,128]{2,1,0:T(8,128)S(1)} all-to-all(f32[16,64,128]{2,1,0:T(8,128)S(1)} %broadcast_in_dim.27), channel_id=1, replica_groups=mesh['dp'=16,'cent'=32] {'dp'}, dimensions={0} | all-to-all | bytes 1048576 | tf_op jit(solution)/shard_map/all_to_all | solution.py:324
  211.8 0.8 copy.100
  (1 shorter events, 0.0 us)
Async XLA Ops:
  0.0 1.0 copy-start.1
  1.0 0.7 copy-start.2
  1.7 0.7 copy-start.3
  124.0 8.2 %copy-start.6 = (f32[32,130,1,128]{3,2,1,0:T(1,128)}, f32[32,130,1,128]{3,2,1,0:T(1,128)S(1)}, u32[]{:S(2)}) copy-start(f32[32,130,1,128]{3,2,1,0:T(1,128)S(1)} %all_to_all.86) | copy-start | bytes 6389764
  132.2 1.7 copy-start
  133.9 54.5 %copy-start.16 = (f32[128]{0:T(128)S(1)}, f32[128]{0:T(128)}, u32[]{:S(2)}) copy-start(f32[128]{0:T(128)} %param.13) | copy-start | bytes 1540
  133.9 54.5 %all-to-all-start.17 = ((f32[16,400,128]{2,1,0:T(8,128)}), f32[16,400,128]{2,1,0:T(8,128)S(1)}, u32[]{:S(2)}, u32[]{:S(2)}) async-start(f32[16,400,128]{2,1,0:T(8,128)} %bitcast.150), calls=%async_computation.17 | async-start | bytes 6553600 | tf_op jit(solution)/shard_map/all_to_all | solution.py:312

commit v2 on v0

v2 whole, which is shorter than its diff:
```python
import functools

import jax
import jax.numpy as jnp
from jax import lax
from jax.experimental import pallas as pl
from jax.experimental.pallas import tpu as pltpu
from jax.sharding import PartitionSpec as P

ITERS = 3
CAP = 192
PITCH = CAP + 8
LANES = 128
LIMIT = 48 * 1024 * 1024

parallel_ratio = 4.0
tiny = 1e-06


def _dot(a, b):
    return jnp.dot(a, b, preferred_element_type=jnp.float32)


def _dot_t(a, b):
    return lax.dot_general(a, b, (((1,), (1,)), ((), ())), preferred_element_type=jnp.float32)


def _halves(x):
    high = x.astype(jnp.bfloat16)
    low = (x - high.astype(jnp.float32)).astype(jnp.bfloat16)
    return high, low


def _iota(shape, dim):
    return lax.broadcasted_iota(jnp.int32, shape, dim)


def _upper():
    return (_iota((LANES, LANES), 0) <= _iota((LANES, LANES), 1)).astype(jnp.bfloat16)


def _places(marks, groups):
    within = _dot(jnp.concatenate(marks, axis=0).astype(jnp.bfloat16), _upper())
    before = jnp.zeros((groups, 1), jnp.float32)
    places = []
    for k, mark in enumerate(marks):
        part = within[k * groups : (k + 1) * groups]
        places.append(jnp.sum(mark * (part + (before - 1.0)), axis=0, keepdims=True))
        before = before + part[:, LANES - 1 :]
    return places, before


def _pack_kernel(peers, slots, held, odd_ref, x_ref, w_ref, t_ref, out_ref):
    rows = x_ref.shape[0]
    high, low = _halves(x_ref[...])
    both = jnp.concatenate([high, low], axis=1)
    w_high, w_low = _halves(w_ref[...])
    first = (_iota((peers, 2 * slots), 1) < slots).astype(jnp.int32)
    label = t_ref[...]
    target = label // held
    local = label - target * held
    marks = (_iota((peers, rows), 0) == target).astype(jnp.float32)
    chunks = [marks[:, k : k + LANES] for k in range(0, rows, LANES)]
    places, _ = _places(chunks, peers)
    place = jnp.concatenate(places, axis=1).astype(jnp.int32)
    l_high, l_low = _halves(local.astype(jnp.float32))
    values = jnp.concatenate(
        [marks * v.astype(jnp.float32) for v in (w_high, w_low, l_high, l_low)], axis=0
    ).astype(jnp.bfloat16)
    at = ((_iota((2 * slots, rows), 0) % slots) == place).astype(jnp.bfloat16)
    notes = _dot_t(values, at)
    weight = notes[:peers] + notes[peers : 2 * peers]
    index = notes[2 * peers : 3 * peers] + notes[3 * peers :]
    notes = jnp.where(first != odd_ref[0], weight, index)
    slot = target * slots + place
    block = 8
    for b in range(0, peers, block):
        take = (_iota((block * slots, rows), 0) + b * slots == slot).astype(jnp.bfloat16)
        got = _dot(take, both)
        got = got[:, :LANES] + got[:, LANES:]
        for t in range(block):
            base = (b + t) * (slots + 1)
            out_ref[base : base + slots, :] = got[t * slots : (t + 1) * slots]
            out_ref[base + slots : base + slots + 1, :] = notes[b + t : b + t + 1]


def _pack(points, weight, labels, odd, peers, slots, held):
    return pl.pallas_call(
        functools.partial(_pack_kernel, peers, slots, held),
        out_shape=jax.ShapeDtypeStruct((peers * (slots + 1), LANES), jnp.float32),
        in_specs=[pl.BlockSpec(memory_space=pltpu.SMEM)] + [pl.BlockSpec(memory_space=pltpu.VMEM)] * 3,
        compiler_params=pltpu.CompilerParams(vmem_limit_bytes=LIMIT),
        name="pack",
    )(odd, points, weight, labels)


def _repack_kernel(peers, slots, held, groups, shift_ref, x_ref, *refs):
    out_refs, (even_ref, odd_ref, both_ref) = refs[:-3], refs[-3:]
    pairs = peers // 2
    rows = peers * slots
    per = held // groups
    first = _iota((pairs, LANES), 1) < slots
    for b in range(peers):
        base = b * (slots + 1)
        high, low = _halves(x_ref[base : base + slots, :])
        both_ref[b * slots : (b + 1) * slots, :LANES] = high
        both_ref[b * slots : (b + 1) * slots, LANES:] = low
        note_ref = odd_ref if b % 2 else even_ref
        note_ref[b // 2 : b // 2 + 1, :] = x_ref[base + slots : base + slots + 1, :]
    even, odd = even_ref[...], odd_ref[...]
    weight = jnp.where(first, even, odd)
    local = pltpu.roll(jnp.where(first, odd, even), slots, 1).astype(jnp.int32)
    owner = local // per - shift_ref[0]
    owner = jnp.where(owner < 0, owner + groups, owner)
    owner = jnp.where(weight > 0.0, owner, -1)
    index = (local % per).astype(jnp.float32)
    marks = [
        (_iota((groups, LANES), 0) == owner[k : k + 1]).astype(jnp.float32) for k in range(pairs)
    ]
    places, sizes = _places(marks, groups)
    flag = jnp.max(sizes, axis=0, keepdims=True) > CAP
    flag = jnp.where(flag, jnp.ones((1, LANES), jnp.float32), 0.0)
    place = jnp.concatenate(places, axis=1).astype(jnp.int32)
    owner = jnp.concatenate([owner[k : k + 1] for k in range(pairs)], axis=1)
    fits = (owner >= 0) & (place < CAP)
    place = jnp.where(fits, place, -1)
    slot = jnp.where(fits, owner * PITCH + place, -1)
    w_high, w_low = _halves(weight)
    values = jnp.concatenate(
        [
            jnp.concatenate([marks[k] * v[k : k + 1] for k in range(pairs)], axis=1)
            for v in (w_high.astype(jnp.float32), w_low.astype(jnp.float32), index)
        ],
        axis=0,
    ).astype(jnp.bfloat16)
    at = (_iota((2 * LANES, rows), 0) == place).astype(jnp.bfloat16)
    notes = _dot_t(values, at)
    weight = notes[:groups] + notes[groups : 2 * groups]
    index = notes[2 * groups :]
    both = both_ref[...]
    for o in range(0, groups, 2):
        take = (_iota((2 * PITCH, rows), 0) + o * PITCH == slot).astype(jnp.bfloat16)
        got = _dot(take, both)
        got = got[:, :LANES] + got[:, LANES:]
        for half in range(2):
            own = o + half
            out_ref, base = (out_refs[own], 0) if len(out_refs) > 1 else (out_refs[0], own * PITCH)
            out_ref[base : base + PITCH, :] = got[half * PITCH : (half + 1) * PITCH]
            base = base + CAP
            out_ref[base : base + 1, :] = weight[own : own + 1, :LANES]
            out_ref[base + 1 : base + 2, :] = weight[own : own + 1, LANES:]
            out_ref[base + 2 : base + 3, :] = index[own : own + 1, :LANES]
            out_ref[base + 3 : base + 4, :] = index[own : own + 1, LANES:]
            out_ref[base + 4 : base + 5, :] = flag


def _repack(got, shift, parts, peers, slots, held, groups):
    return pl.pallas_call(
        functools.partial(_repack_kernel, peers, slots, held, groups),
        out_shape=[jax.ShapeDtypeStruct((groups // parts * PITCH, LANES), jnp.float32)] * parts,
        in_specs=[pl.BlockSpec(memory_space=pltpu.SMEM), pl.BlockSpec(memory_space=pltpu.VMEM)],
        scratch_shapes=[
            pltpu.VMEM((peers // 2, LANES), jnp.float32),
            pltpu.VMEM((peers // 2, LANES), jnp.float32),
            pltpu.VMEM((peers * slots, 2 * LANES), jnp.bfloat16),
        ],
        compiler_params=pltpu.CompilerParams(vmem_limit_bytes=LIMIT),
        name="repack",
    )(shift, got)


def _solve_kernel(groups, cur_ref, prior_ref, seen_ref, *refs):
    x_refs, (out_ref, flag_ref, high_ref, low_ref) = refs[:-4], refs[-4:]
    wide = 2 * LANES
    per = cur_ref.shape[0]
    ones = jnp.ones((8, LANES), jnp.bfloat16)
    flag = seen_ref[...]
    current = cur_ref[...]
    weights, indices, powers = [], [], []
    for s in range(groups):
        x_ref, base = (x_refs[s], 0) if len(x_refs) > 1 else (x_refs[0], s * PITCH)
        rows = x_ref[base : base + CAP, :]
        rows = jnp.concatenate([rows, jnp.zeros((wide - CAP, LANES), jnp.float32)], axis=0)
        high, low = _halves(rows)
        high_ref[s * wide : (s + 1) * wide, :] = high
        low_ref[s * wide : (s + 1) * wide, :] = low
        square_high, square_low = _halves(rows * rows)
        powers.append((_dot_t(ones, square_high) + _dot_t(ones, square_low))[:1])
        notes = x_ref[base + CAP : base + PITCH, :]
        weights += [notes[0:1], notes[1:2]]
        indices += [notes[2:3], notes[3:4]]
        flag = jnp.maximum(flag, notes[4:5])
    weight = jnp.concatenate(weights, axis=1)
    index = jnp.concatenate(indices, axis=1).astype(jnp.int32)
    power = jnp.concatenate(powers, axis=1) * (1.0 / LANES)
    coupling = weight * (parallel_ratio - 1.0) / (LANES * (power + tiny))
    mine = _iota((per, groups * wide), 0) == index
    weighted = jnp.where(mine, weight, 0.0)
    coupled = jnp.where(mine, coupling, 0.0)
    weight_sum = jnp.sum(weighted, axis=1, keepdims=True)
    high, low = high_ref[...], low_ref[...]

    def gather_up(terms):
        a, b = _halves(terms)
        c = _dot(jnp.concatenate([a, b], axis=0), high)
        return c[:per] + c[per:] + _dot(a, low)

    def along(vector):
        a, b = _halves(vector)
        c = _dot_t(jnp.concatenate([a, b], axis=0), high)
        return c[:per] + c[per:] + _dot_t(a, low)

    diagonal = prior_ref[...] + weight_sum
    rhs = prior_ref[...] * current + parallel_ratio * gather_up(weighted)
    current = jnp.zeros_like(rhs)
    residual = rhs
    direction = rhs
    norm_now = jnp.sum(residual * residual, axis=1, keepdims=True)
    for turn in range(ITERS):
        image = diagonal * direction + gather_up(along(direction) * coupled)
        alpha = norm_now / (jnp.sum(direction * image, axis=1, keepdims=True) + tiny)
        current = current + alpha * direction
        if turn + 1 < ITERS:
            residual = residual - alpha * image
            norm_next = jnp.sum(residual * residual, axis=1, keepdims=True)
            direction = residual + (norm_next / (norm_now + tiny)) * direction
            norm_now = norm_next
    out_ref[...] = current
    flag_ref[...] = flag


def _solve(got, current, prior, seen, groups):
    rows = groups * 2 * LANES
    return pl.pallas_call(
        functools.partial(_solve_kernel, groups),
        out_shape=(
            jax.ShapeDtypeStruct(current.shape, jnp.float32),
            jax.ShapeDtypeStruct((1, LANES), jnp.float32),
        ),
        scratch_shapes=[
            pltpu.VMEM((rows, LANES), jnp.bfloat16),
            pltpu.VMEM((rows, LANES), jnp.bfloat16),
        ],
        compiler_params=pltpu.CompilerParams(vmem_limit_bytes=LIMIT),
        name="solve",
    )(current, prior, seen, *got)


def row_terms(vector, got_points, got_weight, got_local, coupling, held):
    picked = jnp.take(vector, got_local, axis=0)
    along = jnp.sum(got_points * picked, axis=1) * coupling
    term = got_weight[:, None] * picked + along[:, None] * got_points
    return jax.ops.segment_sum(term, got_local, num_segments=held)


def dp_sum(x):
    groups = lax.axis_size("dp")
    parts = x.reshape(groups, -1, x.shape[1])
    parts = lax.all_to_all(parts, "dp", split_axis=0, concat_axis=0, tiled=True)
    spread = jnp.broadcast_to(jnp.sum(parts, axis=0)[None], parts.shape)
    return lax.all_to_all(spread, "dp", split_axis=0, concat_axis=0, tiled=True).reshape(x.shape)


def solve_whole(got_points, got_weight, got_local, coupling, current, prior_prec, held):
    data = jax.ops.segment_sum(got_weight[:, None] * got_points, got_local, num_segments=held)
    rhs = prior_prec[None, :] * current + parallel_ratio * dp_sum(data)
    solution = jnp.zeros_like(rhs)
    residual = rhs
    direction = rhs
    norm_now = jnp.sum(residual * residual, axis=1)
    for turn in range(ITERS):
        partial_value = row_terms(direction, got_points, got_weight, got_local, coupling, held)
        image = prior_prec[None, :] * direction + dp_sum(partial_value)
        alpha = norm_now / (jnp.sum(direction * image, axis=1) + tiny)
        solution = solution + alpha[:, None] * direction
        residual = residual - alpha[:, None] * image
        norm_next = jnp.sum(residual * residual, axis=1)
        direction = residual + (norm_next / (norm_now + tiny))[:, None] * direction
        norm_now = norm_next
    return solution


def any_labels(got, centroids, prior_prec, peers, slots):
    held, width = centroids.shape
    current = centroids
    for block in got:
        block = block.reshape(peers, slots + 1, width)
        points = block[:, :slots].reshape(-1, width)
        notes = block[:, slots].reshape(peers // 2, 2, 2, slots)
        weight = jnp.stack([notes[:, 0, 0], notes[:, 1, 1]], axis=1).reshape(-1)
        local = jnp.stack([notes[:, 0, 1], notes[:, 1, 0]], axis=1).reshape(-1).astype(jnp.int32)
        power = jnp.mean(points * points, axis=1)
        coupling = weight * (parallel_ratio - 1.0) / (width * (power + tiny))
        current = solve_whole(points, weight, local, coupling, current, prior_prec, held)
    return current


def per_device(points, row_weight, labels, centroids, prior_prec):
    peers = lax.axis_size("cent")
    groups = lax.axis_size("dp")
    held, width = centroids.shape
    slots = 2 * points.shape[0] // peers
    steps = labels.shape[0]
    per = held // groups
    odd = (lax.axis_index("cent") % 2).reshape(1)
    mine = lax.axis_index("dp")
    start = mine * per
    weight, prior = row_weight.reshape(1, -1), prior_prec.reshape(1, -1)
    got = []
    for step in range(steps):
        sent = _pack(points, weight, labels[step : step + 1], odd, peers, slots, held)
        if got:
            sent, got[-1] = lax.optimization_barrier((sent, got[-1]))
        sent = sent.reshape(peers, slots + 1, 1, width)
        block = lax.all_to_all(sent, "cent", split_axis=0, concat_axis=0, tiled=True)
        got.append(block.reshape(-1, width))
    current = lax.dynamic_slice(centroids, (start, 0), (per, width))
    flag = jnp.zeros((1, LANES), jnp.float32)
    for step in range(steps):
        if step + 1 < steps:
            again = list(_repack(got[step], mine.reshape(1), groups, peers, slots, held, groups))
            for k in range(1, groups):
                again[k] = lax.ppermute(again[k], "dp", [(i, (i + k) % groups) for i in range(groups)])
            again, got[step + 1] = lax.optimization_barrier((again, got[step + 1]))
        else:
            again = _repack(got[step], jnp.zeros((1,), jnp.int32), 1, peers, slots, held, groups)[0]
            again = again.reshape(groups, PITCH, width)
            again = lax.all_to_all(again, "dp", split_axis=0, concat_axis=0, tiled=True)
            again = [again.reshape(-1, width)]
        current, flag = _solve(again, current, prior, flag, groups)

    def summed(got, current):
        every = any_labels(got, centroids, prior_prec, peers, slots)
        return lax.dynamic_slice(every, (start, 0), (per, width))

    current = lax.cond(flag[0, 0] > 0.0, summed, lambda got, current: current, got, current)
    spread = jnp.broadcast_to(current[None], (groups, per, width))
    spread = lax.all_to_all(spread, "dp", split_axis=0, concat_axis=0, tiled=True)
    return spread.reshape(held, width)


def solution(mesh):
    in_specs = (
        P(("dp", "cent"), None),
        P(("dp", "cent")),
        P(None, ("dp", "cent")),
        P("cent", None),
        P(),
    )
    out_specs = P("cent", None)
    return jax.shard_map(
        per_device, mesh=mesh, in_specs=in_specs, out_specs=out_specs, check_vma=False
    )
```

time: 1140 us -> 201 us (0.18)
  the two profiles are of different devices: /device:TPU:1 before, /device:TPU:32 now
where the time goes in v2:
time: 201 us; the launch traced here: 200 us
  starting transfers between devices  87.1 us (43%)
  waiting for transfers between devices  69.5 us (35%)
  Pallas kernels  25.3 us (13%)
  blocking collectives  12.8 us (6%)
  local copies, waits for them, and re-layouts  4.13 us (2%)
    ppermute x15, starting transfers between devices, per_device(): lax.ppermute(again[k], 'dp', [(i, (i + k) % groups) for i in range(groups)])  59.4 us
    all_to_all x2, waiting for transfers between devices, per_device(): lax.all_to_all(sent, 'cent', split_axis=0, concat_axis=0, tiled=True)  52.2 us
    all_to_all x2, starting transfers between devices, per_device(): lax.all_to_all(sent, 'cent', split_axis=0, concat_axis=0, tiled=True)  21.2 us
    all_to_all x1, waiting for transfers between devices, per_device(): again = lax.all_to_all(again, 'dp', split_axis=0, concat_axis=0, tiled=True)  14.5 us
    all_to_all x1, blocking collectives, per_device(): lax.all_to_all(spread, 'dp', split_axis=0, concat_axis=0, tiled=True)  12.8 us
    pallas_call x2, Pallas kernels, _solve(): pl.pallas_call(functools.partial(_solve_kernel, groups), out_shape=(jax.S...  10.5 us
    pallas_call x2, Pallas kernels, _repack(): pl.pallas_call(functools.partial(_repack_kernel, peers, slots, held, grou...  9.66 us
    all_to_all x1, starting transfers between devices, per_device(): again = lax.all_to_all(again, 'dp', split_axis=0, concat_axis=0, tiled=True)  6.49 us
  transfers between devices with their start and end apart: 18, of which 4 were waited for; matrix products, arithmetic and copies ran while one was open for 0% of the time, Pallas kernels for 6%

profile of v2, /device:TPU:32, one launch (start us, length us, event | category | flops | bytes accessed | tf_op | source)
XLA Modules:
  0.0 199.6 jit_solution(17397438669318204713)
XLA Ops:
  5.1 15.5 %all-to-all-start.16 = ((f32[32,65,1,128]{3,2,1,0:T(1,128)}), f32[32,65,1,128]{3,2,1,0:T(1,128)S(1)}, u32[]{:S(2)}, u32[]{:S(2)}) async-start(f32[32,65,1,128]{3,2,1,0:T(1,128)} %bitcast.30), calls=%async_computation.16 | async-start | bytes 2129920 | tf_op jit(solution)/shard_map/all_to_all | solution.py:315
  23.2 52.2 %all-to-all-done.16 = f32[32,65,1,128]{3,2,1,0:T(1,128)S(1)} async-done(((f32[32,65,1,128]{3,2,1,0:T(1,128)}), f32[32,65,1,128]{3,2,1,0:T(1,128)S(1)}, u32[]{:S(2)}, u32[]{:S(2)}) %all-to-all-start.16) | async-done | bytes 1064992 | tf_op jit(solution)/shard_map/all_to_all | solution.py:315
  75.4 5.7 %all-to-all-start.17 = ((f32[32,65,1,128]{3,2,1,0:T(1,128)}), f32[32,65,1,128]{3,2,1,0:T(1,128)S(1)}, u32[]{:S(2)}, u32[]{:S(2)}) async-start(f32[32,65,1,128]{3,2,1,0:T(1,128)} %bitcast.32), calls=%async_computation.17 | async-start | bytes 2129920 | tf_op jit(solution)/shard_map/all_to_all | solution.py:315
  81.1 4.2 %repack.2 = (f32[200,128]{1,0:T(8,128)S(1)}, f32[200,128]{1,0:T(8,128)S(1)}, f32[200,128]{1,0:T(8,128)S(1)}, f32[200,128]{1,0:T(8,128)S(1)}, f32[200,128]{1,0:T(...) custom-call(s32[1]{0:T(128)} %bitcast.27.shift_ref, ...), custom_call_target="tpu_custom_call" | custom-call | tf_op jit(solution)/shard_map/repack/pallas_call | solution.py:158
  85.4 3.4 %collective-permute-start = (f32[200,128]{1,0:T(8,128)S(1)}, f32[200,128]{1,0:T(8,128)S(1)}, u32[]{:S(2)}, u32[]{:S(2)}) collective-permute-start(f32[200,128]{1,0:T(8,128)S(1)} %get-tuple-element.66), channel_id=1, source_target_pairs={{0,32},{32,64},{64,96},{96,128},{128,160},{160,192},{192,224},{224... | collective-permute-start | bytes 307208 | tf_op jit(solution)/shard_map/ppermute | solution.py:323
  88.8 4.6 %collective-permute-start.1 = (f32[200,128]{1,0:T(8,128)S(1)}, f32[200,128]{1,0:T(8,128)S(1)}, u32[]{:S(2)}, u32[]{:S(2)}) collective-permute-start(f32[200,128]{1,0:T(8,128)S(1)} %get-tuple-element.67), channel_id=1, source_target_pairs={{0,64},{32,96},{64,128},{96,160},{128,192},{160,224},{192,256},{22... | collective-permute-start | bytes 307208 | tf_op jit(solution)/shard_map/ppermute | solution.py:323
  93.4 4.4 %collective-permute-start.2 = (f32[200,128]{1,0:T(8,128)S(1)}, f32[200,128]{1,0:T(8,128)S(1)}, u32[]{:S(2)}, u32[]{:S(2)}) collective-permute-start(f32[200,128]{1,0:T(8,128)S(1)} %get-tuple-element.68), channel_id=1, source_target_pairs={{0,96},{32,128},{64,160},{96,192},{128,224},{160,256},{192,288},{2... | collective-permute-start | bytes 307208 | tf_op jit(solution)/shard_map/ppermute | solution.py:323
  97.8 3.5 %collective-permute-start.3 = (f32[200,128]{1,0:T(8,128)S(1)}, f32[200,128]{1,0:T(8,128)S(1)}, u32[]{:S(2)}, u32[]{:S(2)}) collective-permute-start(f32[200,128]{1,0:T(8,128)S(1)} %get-tuple-element.69), channel_id=1, source_target_pairs={{0,128},{32,160},{64,192},{96,224},{128,256},{160,288},{192,320},{... | collective-permute-start | bytes 307208 | tf_op jit(solution)/shard_map/ppermute | solution.py:323
  101.3 3.2 %collective-permute-start.4 = (f32[200,128]{1,0:T(8,128)S(1)}, f32[200,128]{1,0:T(8,128)S(1)}, u32[]{:S(2)}, u32[]{:S(2)}) collective-permute-start(f32[200,128]{1,0:T(8,128)S(1)} %get-tuple-element.70), channel_id=1, source_target_pairs={{0,160},{32,192},{64,224},{96,256},{128,288},{160,320},{192,352},{... | collective-permute-start | bytes 307208 | tf_op jit(solution)/shard_map/ppermute | solution.py:323
  104.5 3.4 %collective-permute-start.5 = (f32[200,128]{1,0:T(8,128)S(1)}, f32[200,128]{1,0:T(8,128)S(1)}, u32[]{:S(2)}, u32[]{:S(2)}) collective-permute-start(f32[200,128]{1,0:T(8,128)S(1)} %get-tuple-element.71), channel_id=1, source_target_pairs={{0,192},{32,224},{64,256},{96,288},{128,320},{160,352},{192,384},{... | collective-permute-start | bytes 307208 | tf_op jit(solution)/shard_map/ppermute | solution.py:323
  107.9 5.4 %collective-permute-start.6 = (f32[200,128]{1,0:T(8,128)S(1)}, f32[200,128]{1,0:T(8,128)S(1)}, u32[]{:S(2)}, u32[]{:S(2)}) collective-permute-start(f32[200,128]{1,0:T(8,128)S(1)} %get-tuple-element.72), channel_id=1, source_target_pairs={{0,224},{32,256},{64,288},{96,320},{128,352},{160,384},{192,416},{... | collective-permute-start | bytes 307208 | tf_op jit(solution)/shard_map/ppermute | solution.py:323
  113.3 3.8 %collective-permute-start.7 = (f32[200,128]{1,0:T(8,128)S(1)}, f32[200,128]{1,0:T(8,128)S(1)}, u32[]{:S(2)}, u32[]{:S(2)}) collective-permute-start(f32[200,128]{1,0:T(8,128)S(1)} %get-tuple-element.73), channel_id=1, source_target_pairs={{0,256},{32,288},{64,320},{96,352},{128,384},{160,416},{192,448},{... | collective-permute-start | bytes 307208 | tf_op jit(solution)/shard_map/ppermute | solution.py:323
  117.1 3.9 %collective-permute-start.8 = (f32[200,128]{1,0:T(8,128)S(1)}, f32[200,128]{1,0:T(8,128)S(1)}, u32[]{:S(2)}, u32[]{:S(2)}) collective-permute-start(f32[200,128]{1,0:T(8,128)S(1)} %get-tuple-element.74), channel_id=1, source_target_pairs={{0,288},{32,320},{64,352},{96,384},{128,416},{160,448},{192,480},{... | collective-permute-start | bytes 307208 | tf_op jit(solution)/shard_map/ppermute | solution.py:323
  121.0 5.3 %collective-permute-start.9 = (f32[200,128]{1,0:T(8,128)S(1)}, f32[200,128]{1,0:T(8,128)S(1)}, u32[]{:S(2)}, u32[]{:S(2)}) collective-permute-start(f32[200,128]{1,0:T(8,128)S(1)} %get-tuple-element.75), channel_id=1, source_target_pairs={{0,320},{32,352},{64,384},{96,416},{128,448},{160,480},{192,0},{22... | collective-permute-start | bytes 307208 | tf_op jit(solution)/shard_map/ppermute | solution.py:323
  126.4 5.0 %collective-permute-start.10 = (f32[200,128]{1,0:T(8,128)S(1)}, f32[200,128]{1,0:T(8,128)S(1)}, u32[]{:S(2)}, u32[]{:S(2)}) collective-permute-start(f32[200,128]{1,0:T(8,128)S(1)} %get-tuple-element.76), channel_id=1, source_target_pairs={{0,352},{32,384},{64,416},{96,448},{128,480},{160,0},{192,32},{224... | collective-permute-start | bytes 307208 | tf_op jit(solution)/shard_map/ppermute | solution.py:323
  131.4 4.3 %collective-permute-start.11 = (f32[200,128]{1,0:T(8,128)S(1)}, f32[200,128]{1,0:T(8,128)S(1)}, u32[]{:S(2)}, u32[]{:S(2)}) collective-permute-start(f32[200,128]{1,0:T(8,128)S(1)} %get-tuple-element.77), channel_id=1, source_target_pairs={{0,384},{32,416},{64,448},{96,480},{128,0},{160,32},{192,64},{224,... | collective-permute-start | bytes 307208 | tf_op jit(solution)/shard_map/ppermute | solution.py:323
  137.7 2.8 %collective-permute-start.13 = (f32[200,128]{1,0:T(8,128)S(1)}, f32[200,128]{1,0:T(8,128)S(1)}, u32[]{:S(2)}, u32[]{:S(2)}) collective-permute-start(f32[200,128]{1,0:T(8,128)S(1)} %get-tuple-element.79), channel_id=1, source_target_pairs={{0,448},{32,480},{64,0},{96,32},{128,64},{160,96},{192,128},{224,1... | collective-permute-start | bytes 307208 | tf_op jit(solution)/shard_map/ppermute | solution.py:323
  140.5 4.5 %collective-permute-start.14 = (f32[200,128]{1,0:T(8,128)S(1)}, f32[200,128]{1,0:T(8,128)S(1)}, u32[]{:S(2)}, u32[]{:S(2)}) collective-permute-start(f32[200,128]{1,0:T(8,128)S(1)} %get-tuple-element.80), channel_id=1, source_target_pairs={{0,480},{32,0},{64,32},{96,64},{128,96},{160,128},{192,160},{224,1... | collective-permute-start | bytes 307208 | tf_op jit(solution)/shard_map/ppermute | solution.py:323
  147.8 5.4 %repack.3 = f32[3200,128]{1,0:T(8,128)} custom-call(s32[1]{0:T(128)} %constant.61.clone.1.shift_ref, f32[2080,128]{1,0:T(8,128)S(1)} %bitcast.147), custom_call_target="tpu_custom_call" | custom-call | tf_op jit(solution)/shard_map/repack/pallas_call | solution.py:158
  153.3 6.5 %all-to-all-start.18 = ((f32[16,200,128]{2,1,0:T(8,128)}), f32[16,200,128]{2,1,0:T(8,128)S(1)}, u32[]{:S(2)}, u32[]{:S(2)}) async-start(f32[16,200,128]{2,1,0:T(8,128)} %bitcast.34), calls=%async_computation.18 | async-start | bytes 3276800 | tf_op jit(solution)/shard_map/all_to_all | solution.py:328
  160.5 5.3 %solve.2 = (f32[64,128]{1,0:T(8,128)S(1)}, f32[1,128]{1,0:T(1,128)S(1)}) custom-call(f32[64,128]{1,0:T(8,128)S(1)} %constant_dynamic-slice_fusion.cur_ref, f32[1,128]{1,0:T(1,128)S(1)} %bitcast.159, f32[1,128]{1,0:T(1,128)S(1)} %broadcast_in_dim.29.seen_ref, f32[200,128]{1,0:T(8,128)S(1)} %get-tuple-element.82.refs_0_, ...), custom_call_target="tpu_custom_call" | custom-call | tf_op jit(solution)/shard_map/solve/pallas_call | solution.py:234
  165.8 14.5 %all-to-all-done.18 = f32[16,200,128]{2,1,0:T(8,128)S(1)} async-done(((f32[16,200,128]{2,1,0:T(8,128)}), f32[16,200,128]{2,1,0:T(8,128)S(1)}, u32[]{:S(2)}, u32[]{:S(2)}) %all-to-all-start.18) | async-done | bytes 1638432 | tf_op jit(solution)/shard_map/all_to_all | solution.py:328
  180.3 5.2 %solve.3 = (f32[64,128]{1,0:T(8,128)S(1)}, f32[1,128]{1,0:T(1,128)S(1)}) custom-call(f32[64,128]{1,0:T(8,128)S(1)} %get-tuple-element.98.cur_ref, f32[1,128]{1,0:T(1,128)S(1)} %bitcast.160, f32[1,128]{1,0:T(1,128)S(1)} %get-tuple-element.99.seen_ref, f32[3200,128]{1,0:T(8,128)S(1)} %bitcast.143), custom_call_target="tpu_custom_call" | custom-call | tf_op jit(solution)/shard_map/solve/pallas_call | solution.py:234
  186.0 12.8 %all_to_all.91 = f32[16,64,128]{2,1,0:T(8,128)S(1)} all-to-all(f32[16,64,128]{2,1,0:T(8,128)S(1)} %broadcast_in_dim.30), channel_id=1, replica_groups=mesh['dp'=16,'cent'=32] {'dp'}, dimensions={0} | all-to-all | bytes 1048576 | tf_op jit(solution)/shard_map/all_to_all | solution.py:338
  (41 shorter events, 14.3 us)
Async XLA Ops:
  5.1 15.5 %copy-start.1 = (f32[1024,128]{1,0:T(8,128)S(1)}, f32[1024,128]{1,0:T(8,128)}, u32[]{:S(2)}) copy-start(f32[1024,128]{1,0:T(8,128)} %x_ref.3) | copy-start | bytes 1572868
  5.1 15.5 %copy-start.3 = (f32[1024]{0:T(1024)S(1)}, f32[1024]{0:T(1024)}, u32[]{:S(2)}) copy-start(f32[1024]{0:T(1024)} %param.10) | copy-start | bytes 12292
  5.1 70.3 %all-to-all-start.16 = ((f32[32,65,1,128]{3,2,1,0:T(1,128)}), f32[32,65,1,128]{3,2,1,0:T(1,128)S(1)}, u32[]{:S(2)}, u32[]{:S(2)}) async-start(f32[32,65,1,128]{3,2,1,0:T(1,128)} %bitcast.30), calls=%async_computation.16 | async-start | bytes 2129920 | tf_op jit(solution)/shard_map/all_to_all | solution.py:315
  75.4 10.0 %copy-start.8 = (f32[32,65,1,128]{3,2,1,0:T(1,128)}, f32[32,65,1,128]{3,2,1,0:T(1,128)S(1)}, u32[]{:S(2)}) copy-start(f32[32,65,1,128]{3,2,1,0:T(1,128)S(1)} %all-to-all-done.16) | copy-start | bytes 3194884
  75.4 72.4 %all-to-all-start.17 = ((f32[32,65,1,128]{3,2,1,0:T(1,128)}), f32[32,65,1,128]{3,2,1,0:T(1,128)S(1)}, u32[]{:S(2)}, u32[]{:S(2)}) async-start(f32[32,65,1,128]{3,2,1,0:T(1,128)} %bitcast.32), calls=%async_computation.17 | async-start | bytes 2129920 | tf_op jit(solution)/shard_map/all_to_all | solution.py:315
  85.4 19.1 %collective-permute-start = (f32[200,128]{1,0:T(8,128)S(1)}, f32[200,128]{1,0:T(8,128)S(1)}, u32[]{:S(2)}, u32[]{:S(2)}) collective-permute-start(f32[200,128]{1,0:T(8,128)S(1)} %get-tuple-element.66), channel_id=1, source_target_pairs={{0,32},{32,64},{64,96},{96,128},{128,160},{160,192},{192,224},{224... | collective-permute-start | bytes 307208 | tf_op jit(solution)/shard_map/ppermute | solution.py:323
  88.8 19.1 %collective-permute-start.1 = (f32[200,128]{1,0:T(8,128)S(1)}, f32[200,128]{1,0:T(8,128)S(1)}, u32[]{:S(2)}, u32[]{:S(2)}) collective-permute-start(f32[200,128]{1,0:T(8,128)S(1)} %get-tuple-element.67), channel_id=1, source_target_pairs={{0,64},{32,96},{64,128},{96,160},{128,192},{160,224},{192,256},{22... | collective-permute-start | bytes 307208 | tf_op jit(solution)/shard_map/ppermute | solution.py:323
  93.4 19.9 %collective-permute-start.2 = (f32[200,128]{1,0:T(8,128)S(1)}, f32[200,128]{1,0:T(8,128)S(1)}, u32[]{:S(2)}, u32[]{:S(2)}) collective-permute-start(f32[200,128]{1,0:T(8,128)S(1)} %get-tuple-element.68), channel_id=1, source_target_pairs={{0,96},{32,128},{64,160},{96,192},{128,224},{160,256},{192,288},{2... | collective-permute-start | bytes 307208 | tf_op jit(solution)/shard_map/ppermute | solution.py:323
  97.8 19.3 %collective-permute-start.3 = (f32[200,128]{1,0:T(8,128)S(1)}, f32[200,128]{1,0:T(8,128)S(1)}, u32[]{:S(2)}, u32[]{:S(2)}) collective-permute-start(f32[200,128]{1,0:T(8,128)S(1)} %get-tuple-element.69), channel_id=1, source_target_pairs={{0,128},{32,160},{64,192},{96,224},{128,256},{160,288},{192,320},{... | collective-permute-start | bytes 307208 | tf_op jit(solution)/shard_map/ppermute | solution.py:323
  101.3 19.7 %collective-permute-start.4 = (f32[200,128]{1,0:T(8,128)S(1)}, f32[200,128]{1,0:T(8,128)S(1)}, u32[]{:S(2)}, u32[]{:S(2)}) collective-permute-start(f32[200,128]{1,0:T(8,128)S(1)} %get-tuple-element.70), channel_id=1, source_target_pairs={{0,160},{32,192},{64,224},{96,256},{128,288},{160,320},{192,352},{... | collective-permute-start | bytes 307208 | tf_op jit(solution)/shard_map/ppermute | solution.py:323
  104.5 21.8 %collective-permute-start.5 = (f32[200,128]{1,0:T(8,128)S(1)}, f32[200,128]{1,0:T(8,128)S(1)}, u32[]{:S(2)}, u32[]{:S(2)}) collective-permute-start(f32[200,128]{1,0:T(8,128)S(1)} %get-tuple-element.71), channel_id=1, source_target_pairs={{0,192},{32,224},{64,256},{96,288},{128,320},{160,352},{192,384},{... | collective-permute-start | bytes 307208 | tf_op jit(solution)/shard_map/ppermute | solution.py:323
  107.9 23.5 %collective-permute-start.6 = (f32[200,128]{1,0:T(8,128)S(1)}, f32[200,128]{1,0:T(8,128)S(1)}, u32[]{:S(2)}, u32[]{:S(2)}) collective-permute-start(f32[200,128]{1,0:T(8,128)S(1)} %get-tuple-element.72), channel_id=1, source_target_pairs={{0,224},{32,256},{64,288},{96,320},{128,352},{160,384},{192,416},{... | collective-permute-start | bytes 307208 | tf_op jit(solution)/shard_map/ppermute | solution.py:323
  113.3 22.4 %collective-permute-start.7 = (f32[200,128]{1,0:T(8,128)S(1)}, f32[200,128]{1,0:T(8,128)S(1)}, u32[]{:S(2)}, u32[]{:S(2)}) collective-permute-start(f32[200,128]{1,0:T(8,128)S(1)} %get-tuple-element.73), channel_id=1, source_target_pairs={{0,256},{32,288},{64,320},{96,352},{128,384},{160,416},{192,448},{... | collective-permute-start | bytes 307208 | tf_op jit(solution)/shard_map/ppermute | solution.py:323
  117.1 20.6 %collective-permute-start.8 = (f32[200,128]{1,0:T(8,128)S(1)}, f32[200,128]{1,0:T(8,128)S(1)}, u32[]{:S(2)}, u32[]{:S(2)}) collective-permute-start(f32[200,128]{1,0:T(8,128)S(1)} %get-tuple-element.74), channel_id=1, source_target_pairs={{0,288},{32,320},{64,352},{96,384},{128,416},{160,448},{192,480},{... | collective-permute-start | bytes 307208 | tf_op jit(solution)/shard_map/ppermute | solution.py:323
  121.0 19.4 %collective-permute-start.9 = (f32[200,128]{1,0:T(8,128)S(1)}, f32[200,128]{1,0:T(8,128)S(1)}, u32[]{:S(2)}, u32[]{:S(2)}) collective-permute-start(f32[200,128]{1,0:T(8,128)S(1)} %get-tuple-element.75), channel_id=1, source_target_pairs={{0,320},{32,352},{64,384},{96,416},{128,448},{160,480},{192,0},{22... | collective-permute-start | bytes 307208 | tf_op jit(solution)/shard_map/ppermute | solution.py:323
  126.4 18.7 %collective-permute-start.10 = (f32[200,128]{1,0:T(8,128)S(1)}, f32[200,128]{1,0:T(8,128)S(1)}, u32[]{:S(2)}, u32[]{:S(2)}) collective-permute-start(f32[200,128]{1,0:T(8,128)S(1)} %get-tuple-element.76), channel_id=1, source_target_pairs={{0,352},{32,384},{64,416},{96,448},{128,480},{160,0},{192,32},{224... | collective-permute-start | bytes 307208 | tf_op jit(solution)/shard_map/ppermute | solution.py:323
  131.4 13.6 %collective-permute-start.11 = (f32[200,128]{1,0:T(8,128)S(1)}, f32[200,128]{1,0:T(8,128)S(1)}, u32[]{:S(2)}, u32[]{:S(2)}) collective-permute-start(f32[200,128]{1,0:T(8,128)S(1)} %get-tuple-element.77), channel_id=1, source_target_pairs={{0,384},{32,416},{64,448},{96,480},{128,0},{160,32},{192,64},{224,... | collective-permute-start | bytes 307208 | tf_op jit(solution)/shard_map/ppermute | solution.py:323
  135.8 9.3 %collective-permute-start.12 = (f32[200,128]{1,0:T(8,128)S(1)}, f32[200,128]{1,0:T(8,128)S(1)}, u32[]{:S(2)}, u32[]{:S(2)}) collective-permute-start(f32[200,128]{1,0:T(8,128)S(1)} %get-tuple-element.78), channel_id=1, source_target_pairs={{0,416},{32,448},{64,480},{96,0},{128,32},{160,64},{192,96},{224,1... | collective-permute-start | bytes 307208 | tf_op jit(solution)/shard_map/ppermute | solution.py:323
  137.7 8.1 %collective-permute-start.13 = (f32[200,128]{1,0:T(8,128)S(1)}, f32[200,128]{1,0:T(8,128)S(1)}, u32[]{:S(2)}, u32[]{:S(2)}) collective-permute-start(f32[200,128]{1,0:T(8,128)S(1)} %get-tuple-element.79), channel_id=1, source_target_pairs={{0,448},{32,480},{64,0},{96,32},{128,64},{160,96},{192,128},{224,1... | collective-permute-start | bytes 307208 | tf_op jit(solution)/shard_map/ppermute | solution.py:323
  140.5 7.3 %collective-permute-start.14 = (f32[200,128]{1,0:T(8,128)S(1)}, f32[200,128]{1,0:T(8,128)S(1)}, u32[]{:S(2)}, u32[]{:S(2)}) collective-permute-start(f32[200,128]{1,0:T(8,128)S(1)} %get-tuple-element.80), channel_id=1, source_target_pairs={{0,480},{32,0},{64,32},{96,64},{128,96},{160,128},{192,160},{224,1... | collective-permute-start | bytes 307208 | tf_op jit(solution)/shard_map/ppermute | solution.py:323
  147.8 5.4 %copy-start.6 = (f32[32,65,1,128]{3,2,1,0:T(1,128)}, f32[32,65,1,128]{3,2,1,0:T(1,128)S(1)}, u32[]{:S(2)}) copy-start(f32[32,65,1,128]{3,2,1,0:T(1,128)S(1)} %all-to-all-done.17) | copy-start | bytes 3194884
  153.3 7.3 %copy-start.20 = (f32[128]{0:T(128)S(1)}, f32[128]{0:T(128)}, u32[]{:S(2)}) copy-start(f32[128]{0:T(128)} %param.13) | copy-start | bytes 1540
  153.3 27.1 %all-to-all-start.18 = ((f32[16,200,128]{2,1,0:T(8,128)}), f32[16,200,128]{2,1,0:T(8,128)S(1)}, u32[]{:S(2)}, u32[]{:S(2)}) async-start(f32[16,200,128]{2,1,0:T(8,128)} %bitcast.34), calls=%async_computation.18 | async-start | bytes 3276800 | tf_op jit(solution)/shard_map/all_to_all | solution.py:328
  165.8 19.8 %copy-start.9 = (f32[32,65,1,128]{3,2,1,0:T(1,128)S(1)}, f32[32,65,1,128]{3,2,1,0:T(1,128)}, u32[]{:S(2)}) copy-start(f32[32,65,1,128]{3,2,1,0:T(1,128)} %copy-done.8) | copy-start | bytes 3194884
  (2 other events, 1.7 us)

commit v3 on v2

--- a/solution.py
+++ b/solution.py
@@ -1,4 +1,5 @@
 import functools
+import math
 
 import jax
 import jax.numpy as jnp
@@ -8,10 +9,11 @@
 from jax.sharding import PartitionSpec as P
 
 ITERS = 3
-CAP = 192
+CAP = 168
+HALF = 80
 PITCH = CAP + 8
 LANES = 128
-LIMIT = 48 * 1024 * 1024
+LIMIT = 24 * 1024 * 1024
 
 parallel_ratio = 4.0
 tiny = 1e-06
@@ -33,6 +35,14 @@
 
 def _iota(shape, dim):
     return lax.broadcasted_iota(jnp.int32, shape, dim)
+
+
+def _ramp(rows, columns):
+    return _iota((rows, columns), 0).astype(jnp.float32).astype(jnp.bfloat16)
+
+
+def _hits(ramp, places):
+    return jnp.where(ramp == places.astype(jnp.bfloat16), jnp.ones_like(ramp), jnp.zeros_like(ramp))
 
 
 def _upper():
@@ -62,20 +72,22 @@
     marks = (_iota((peers, rows), 0) == target).astype(jnp.float32)
     chunks = [marks[:, k : k + LANES] for k in range(0, rows, LANES)]
     places, _ = _places(chunks, peers)
-    place = jnp.concatenate(places, axis=1).astype(jnp.int32)
+    place = jnp.concatenate(places, axis=1)
     l_high, l_low = _halves(local.astype(jnp.float32))
     values = jnp.concatenate(
         [marks * v.astype(jnp.float32) for v in (w_high, w_low, l_high, l_low)], axis=0
     ).astype(jnp.bfloat16)
-    at = ((_iota((2 * slots, rows), 0) % slots) == place).astype(jnp.bfloat16)
+    ramp = _ramp(slots, rows)
+    at = _hits(ramp, place)
+    at = jnp.concatenate([at, at], axis=0)
     notes = _dot_t(values, at)
     weight = notes[:peers] + notes[peers : 2 * peers]
     index = notes[2 * peers : 3 * peers] + notes[3 * peers :]
     notes = jnp.where(first != odd_ref[0], weight, index)
-    slot = target * slots + place
+    placed = jnp.where(marks > 0.0, place, -1.0)
     block = 8
     for b in range(0, peers, block):
-        take = (_iota((block * slots, rows), 0) + b * slots == slot).astype(jnp.bfloat16)
+        take = jnp.concatenate([_hits(ramp, placed[t : t + 1]) for t in range(b, b + block)], axis=0)
         got = _dot(take, both)
         got = got[:, :LANES] + got[:, LANES:]
         for t in range(block):
@@ -94,8 +106,20 @@
     )(odd, points, weight, labels)
 
 
-def _repack_kernel(peers, slots, held, groups, shift_ref, x_ref, *refs):
+def _sources(groups):
+    side = math.isqrt(groups)
+    table = []
+    for k in range(side):
+        for j in range(side):
+            one = (k, 0, HALF) if j == 0 else (side + j - 1, k * HALF, HALF)
+            two = (2 * side - 1 + j, 0) if k == 0 else (3 * side - 2 + k, j * (PITCH - HALF))
+            table.append(((one, two + (CAP - HALF,)), (two[0], two[1] + CAP - HALF)))
+    return tuple(table)
+
+
+def _repack_kernel(peers, slots, held, groups, me_ref, x_ref, *refs):
     out_refs, (even_ref, odd_ref, both_ref) = refs[:-3], refs[-3:]
+    side = math.isqrt(groups)
     pairs = peers // 2
     rows = peers * slots
     per = held // groups
@@ -110,8 +134,13 @@
     even, odd = even_ref[...], odd_ref[...]
     weight = jnp.where(first, even, odd)
     local = pltpu.roll(jnp.where(first, odd, even), slots, 1).astype(jnp.int32)
-    owner = local // per - shift_ref[0]
-    owner = jnp.where(owner < 0, owner + groups, owner)
+    owner = local // per
+    if len(out_refs) > 1:
+        far_x = owner % side - me_ref[0] % side
+        far_y = owner // side - me_ref[0] // side
+        far_x = jnp.where(far_x < 0, far_x + side, far_x)
+        far_y = jnp.where(far_y < 0, far_y + side, far_y)
+        owner = far_x * side + far_y
     owner = jnp.where(weight > 0.0, owner, -1)
     index = (local % per).astype(jnp.float32)
     marks = [
@@ -120,33 +149,42 @@
     places, sizes = _places(marks, groups)
     flag = jnp.max(sizes, axis=0, keepdims=True) > CAP
     flag = jnp.where(flag, jnp.ones((1, LANES), jnp.float32), 0.0)
-    place = jnp.concatenate(places, axis=1).astype(jnp.int32)
-    owner = jnp.concatenate([owner[k : k + 1] for k in range(pairs)], axis=1)
-    fits = (owner >= 0) & (place < CAP)
-    place = jnp.where(fits, place, -1)
-    slot = jnp.where(fits, owner * PITCH + place, -1)
+    place = jnp.concatenate(places, axis=1)
+    place = jnp.where(place < CAP, place, -1.0)
+    marks = jnp.concatenate(marks, axis=1)
+    placed = jnp.where(marks > 0.0, place, -1.0)
     w_high, w_low = _halves(weight)
     values = jnp.concatenate(
         [
-            jnp.concatenate([marks[k] * v[k : k + 1] for k in range(pairs)], axis=1)
+            marks * jnp.concatenate([v[k : k + 1] for k in range(pairs)], axis=1)
             for v in (w_high.astype(jnp.float32), w_low.astype(jnp.float32), index)
         ],
         axis=0,
     ).astype(jnp.bfloat16)
-    at = (_iota((2 * LANES, rows), 0) == place).astype(jnp.bfloat16)
+    ramp = _ramp(2 * LANES, rows)
+    at = _hits(ramp, place)
     notes = _dot_t(values, at)
     weight = notes[:groups] + notes[groups : 2 * groups]
     index = notes[2 * groups :]
     both = both_ref[...]
     for o in range(0, groups, 2):
-        take = (_iota((2 * PITCH, rows), 0) + o * PITCH == slot).astype(jnp.bfloat16)
+        take = [_hits(ramp[:PITCH], placed[i : i + 1]) for i in range(o, o + 2)]
+        take = jnp.concatenate(take, axis=0)
         got = _dot(take, both)
         got = got[:, :LANES] + got[:, LANES:]
         for half in range(2):
             own = o + half
-            out_ref, base = (out_refs[own], 0) if len(out_refs) > 1 else (out_refs[0], own * PITCH)
-            out_ref[base : base + PITCH, :] = got[half * PITCH : (half + 1) * PITCH]
-            base = base + CAP
+            rows_of = got[half * PITCH : (half + 1) * PITCH]
+            if len(out_refs) > 1:
+                k, j = own // side, own % side
+                out_refs[k][j * HALF : (j + 1) * HALF, :] = rows_of[:HALF]
+                out_ref, base = out_refs[side + j], k * (PITCH - HALF)
+                out_ref[base : base + PITCH - HALF, :] = rows_of[HALF:]
+                base = base + CAP - HALF
+            else:
+                out_ref, base = out_refs[0], own * PITCH
+                out_ref[base : base + PITCH, :] = rows_of
+                base = base + CAP
             out_ref[base : base + 1, :] = weight[own : own + 1, :LANES]
             out_ref[base + 1 : base + 2, :] = weight[own : own + 1, LANES:]
             out_ref[base + 2 : base + 3, :] = index[own : own + 1, :LANES]
@@ -154,10 +192,12 @@
             out_ref[base + 4 : base + 5, :] = flag
 
 
-def _repack(got, shift, parts, peers, slots, held, groups):
+def _repack(got, me, split, peers, slots, held, groups):
+    side = math.isqrt(groups)
+    shapes = [side * HALF] * side + [side * (PITCH - HALF)] * side if split else [groups * PITCH]
     return pl.pallas_call(
         functools.partial(_repack_kernel, peers, slots, held, groups),
-        out_shape=[jax.ShapeDtypeStruct((groups // parts * PITCH, LANES), jnp.float32)] * parts,
+        out_shape=[jax.ShapeDtypeStruct((rows, LANES), jnp.float32) for rows in shapes],
         in_specs=[pl.BlockSpec(memory_space=pltpu.SMEM), pl.BlockSpec(memory_space=pltpu.VMEM)],
         scratch_shapes=[
             pltpu.VMEM((peers // 2, LANES), jnp.float32),
@@ -166,27 +206,26 @@
         ],
         compiler_params=pltpu.CompilerParams(vmem_limit_bytes=LIMIT),
         name="repack",
-    )(shift, got)
-
-
-def _solve_kernel(groups, cur_ref, prior_ref, seen_ref, *refs):
-    x_refs, (out_ref, flag_ref, high_ref, low_ref) = refs[:-4], refs[-4:]
+    )(me, got)
+
+
+def _solve_kernel(table, cur_ref, prior_ref, seen_ref, *refs):
+    x_refs, (out_ref, flag_ref, both_ref) = refs[:-3], refs[-3:]
     wide = 2 * LANES
     per = cur_ref.shape[0]
-    ones = jnp.ones((8, LANES), jnp.bfloat16)
+    ones = jnp.ones((8, 2 * LANES), jnp.bfloat16)
     flag = seen_ref[...]
     current = cur_ref[...]
     weights, indices, powers = [], [], []
-    for s in range(groups):
-        x_ref, base = (x_refs[s], 0) if len(x_refs) > 1 else (x_refs[0], s * PITCH)
-        rows = x_ref[base : base + CAP, :]
-        rows = jnp.concatenate([rows, jnp.zeros((wide - CAP, LANES), jnp.float32)], axis=0)
+    groups = len(table)
+    for s, (parts, (note, first)) in enumerate(table):
+        rows = [x_refs[ref][base : base + count, :] for ref, base, count in parts]
+        rows = jnp.concatenate(rows + [jnp.zeros((wide - CAP, LANES), jnp.float32)], axis=0)
         high, low = _halves(rows)
-        high_ref[s * wide : (s + 1) * wide, :] = high
-        low_ref[s * wide : (s + 1) * wide, :] = low
-        square_high, square_low = _halves(rows * rows)
-        powers.append((_dot_t(ones, square_high) + _dot_t(ones, square_low))[:1])
-        notes = x_ref[base + CAP : base + PITCH, :]
+        both_ref[s * wide : (s + 1) * wide, :LANES] = high
+        both_ref[s * wide : (s + 1) * wide, LANES:] = low
+        powers.append(_dot_t(ones, jnp.concatenate(_halves(rows * rows), axis=1))[:1])
+        notes = x_refs[note][first : first + PITCH - CAP, :]
         weights += [notes[0:1], notes[1:2]]
         indices += [notes[2:3], notes[3:4]]
         flag = jnp.maximum(flag, notes[4:5])
@@ -198,17 +237,17 @@
     weighted = jnp.where(mine, weight, 0.0)
     coupled = jnp.where(mine, coupling, 0.0)
     weight_sum = jnp.sum(weighted, axis=1, keepdims=True)
-    high, low = high_ref[...], low_ref[...]
+    both = both_ref[...]
 
     def gather_up(terms):
-        a, b = _halves(terms)
-        c = _dot(jnp.concatenate([a, b], axis=0), high)
-        return c[:per] + c[per:] + _dot(a, low)
+        c = _dot(jnp.concatenate(_halves(terms), axis=0), both)
+        c = c[:, :LANES] + c[:, LANES:]
+        return c[:per] + c[per:]
 
     def along(vector):
-        a, b = _halves(vector)
-        c = _dot_t(jnp.concatenate([a, b], axis=0), high)
-        return c[:per] + c[per:] + _dot_t(a, low)
+        c = jnp.concatenate(_halves(vector), axis=0)
+        c = _dot_t(jnp.concatenate([c, c], axis=1), both)
+        return c[:per] + c[per:]
 
     diagonal = prior_ref[...] + weight_sum
     rhs = prior_ref[...] * current + parallel_ratio * gather_up(weighted)
@@ -229,17 +268,16 @@
     flag_ref[...] = flag
 
 
-def _solve(got, current, prior, seen, groups):
-    rows = groups * 2 * LANES
+def _solve(got, current, prior, seen, table):
+    rows = len(table) * 2 * LANES
     return pl.pallas_call(
-        functools.partial(_solve_kernel, groups),
+        functools.partial(_solve_kernel, table),
         out_shape=(
             jax.ShapeDtypeStruct(current.shape, jnp.float32),
             jax.ShapeDtypeStruct((1, LANES), jnp.float32),
         ),
         scratch_shapes=[
-            pltpu.VMEM((rows, LANES), jnp.bfloat16),
-            pltpu.VMEM((rows, LANES), jnp.bfloat16),
+            pltpu.VMEM((rows, 2 * LANES), jnp.bfloat16),
         ],
         compiler_params=pltpu.CompilerParams(vmem_limit_bytes=LIMIT),
         name="solve",
@@ -293,6 +331,31 @@
         coupling = weight * (parallel_ratio - 1.0) / (width * (power + tiny))
         current = solve_whole(points, weight, local, coupling, current, prior_prec, held)
     return current
+
+
+def _spread(blocks, groups):
+    side = math.isqrt(groups)
+
+    def move(x, k, along_x):
+        def to(i):
+            y, x = divmod(i, side)
+            return y * side + (x + k) % side if along_x else (y + k) % side * side + x
+
+        return lax.ppermute(x, "dp", [(i, to(i)) for i in range(groups)]) if k else x
+
+    first, second = blocks[:side], blocks[side:]
+    once_1, once_2 = [first[0]], [second[0]]
+    for k in range(1, side):
+        once_1.append(move(first[k], k, True))
+        once_2.append(move(second[k], k, False))
+    twice_1, twice_2 = [], []
+    for k in range(1, side):
+        a, b = k * HALF, k * (PITCH - HALF)
+        both = jnp.concatenate([x[a : a + HALF] for x in once_1], axis=0)
+        twice_1.append(move(both, k, False))
+        both = jnp.concatenate([x[b : b + PITCH - HALF] for x in once_2], axis=0)
+        twice_2.append(move(both, k, True))
+    return once_1 + twice_1 + once_2 + twice_2
 
 
 def per_device(points, row_weight, labels, centroids, prior_prec):
@@ -316,18 +379,18 @@
         got.append(block.reshape(-1, width))
     current = lax.dynamic_slice(centroids, (start, 0), (per, width))
     flag = jnp.zeros((1, LANES), jnp.float32)
+    args = peers, slots, held, groups
     for step in range(steps):
         if step + 1 < steps:
-            again = list(_repack(got[step], mine.reshape(1), groups, peers, slots, held, groups))
-            for k in range(1, groups):
-                again[k] = lax.ppermute(again[k], "dp", [(i, (i + k) % groups) for i in range(groups)])
+            again = _spread(_repack(got[step], mine.reshape(1), True, *args), groups)
             again, got[step + 1] = lax.optimization_barrier((again, got[step + 1]))
+            table = _sources(groups)
         else:
-            again = _repack(got[step], jnp.zeros((1,), jnp.int32), 1, peers, slots, held, groups)[0]
-            again = again.reshape(groups, PITCH, width)
+            again = _repack(got[step], mine.reshape(1), False, *args)[0].reshape(groups, PITCH, width)
             again = lax.all_to_all(again, "dp", split_axis=0, concat_axis=0, tiled=True)
             again = [again.reshape(-1, width)]
-        current, flag = _solve(again, current, prior, flag, groups)
+            table = tuple((((0, s * PITCH, CAP),), (0, s * PITCH + CAP)) for s in range(groups))
+        current, flag = _solve(again, current, prior, flag, table)
 
     def summed(got, current):
         every = any_labels(got, centroids, prior_prec, peers, slots)

time: 201 us -> 194 us (0.965)
  the two profiles are of different devices: /device:TPU:32 before, /device:TPU:1 now
where the time goes in v3:
time: 194 us; the launch traced here: 193 us
  waiting for transfers between devices  77.1 us (40%)
  starting transfers between devices  66.1 us (34%)
  Pallas kernels  23.9 us (12%)
  blocking collectives  16.3 us (8%)
  local copies, waits for them, and re-layouts  8.94 us (5%)
    all_to_all x2, waiting for transfers between devices, per_device(): lax.all_to_all(sent, 'cent', split_axis=0, concat_axis=0, tiled=True)  62.7 us
    ppermute x12, starting transfers between devices, move(): lax.ppermute(x, 'dp', [(i, to(i)) for i in range(groups)])  38.2 us
    all_to_all x2, starting transfers between devices, per_device(): lax.all_to_all(sent, 'cent', split_axis=0, concat_axis=0, tiled=True)  21 us
    all_to_all x1, blocking collectives, per_device(): lax.all_to_all(spread, 'dp', split_axis=0, concat_axis=0, tiled=True)  16.3 us
    all_to_all x1, waiting for transfers between devices, per_device(): again = lax.all_to_all(again, 'dp', split_axis=0, concat_axis=0, tiled=True)  11.2 us
    pallas_call x2, Pallas kernels, _solve(): pl.pallas_call(functools.partial(_solve_kernel, table), out_shape=(jax.Sh...  10.1 us
    pallas_call x2, Pallas kernels, _repack(): pl.pallas_call(functools.partial(_repack_kernel, peers, slots, held, grou...  8.7 us
    unnamed x29, local copies, waits for them, and re-layouts  7.26 us
  transfers between devices with their start and end apart: 15, of which 4 were waited for; matrix products, arithmetic and copies ran while one was open for 0% of the time, Pallas kernels for 6%

profile of v3, /device:TPU:1, one launch (start us, length us, event | category | flops | bytes accessed | tf_op | source)
XLA Modules:
  0.0 193.1 jit_solution(16016881904910493809)
XLA Ops:
  2.5 2.6 %pack.3 = f32[2080,128]{1,0:T(8,128)} custom-call(s32[1]{0:T(128)} %bitcast.28.odd_ref, f32[1024,128]{1,0:T(8,128)S(1)} %copy-done, f32[1,1024]{1,0:T(1,128)S(1)} %bitcast.144, s32[1,1024]{1,0:T(1,128)S(1)} %get-tuple-element.129.t_ref), custom_call_target="tpu_custom_call" | custom-call | tf_op jit(solution)/shard_map/pack/pallas_call | solution.py:100
  5.1 16.9 %all-to-all-start.16 = ((f32[32,65,1,128]{3,2,1,0:T(1,128)}), f32[32,65,1,128]{3,2,1,0:T(1,128)S(1)}, u32[]{:S(2)}, u32[]{:S(2)}) async-start(f32[32,65,1,128]{3,2,1,0:T(1,128)} %bitcast.30), calls=%async_computation.16 | async-start | bytes 2129920 | tf_op jit(solution)/shard_map/all_to_all | solution.py:378
  22.0 2.5 %pack.2 = f32[2080,128]{1,0:T(8,128)} custom-call(s32[1]{0:T(128)} %bitcast.28.odd_ref, f32[1024,128]{1,0:T(8,128)S(1)} %copy-done.1, f32[1,1024]{1,0:T(1,128)S(1)} %bitcast.145, s32[1,1024]{1,0:T(1,128)S(1)} %get-tuple-element.130.t_ref), custom_call_target="tpu_custom_call" | custom-call | tf_op jit(solution)/shard_map/pack/pallas_call | solution.py:100
  24.5 53.9 %all-to-all-done.16 = f32[32,65,1,128]{3,2,1,0:T(1,128)S(1)} async-done(((f32[32,65,1,128]{3,2,1,0:T(1,128)}), f32[32,65,1,128]{3,2,1,0:T(1,128)S(1)}, u32[]{:S(2)}, u32[]{:S(2)}) %all-to-all-start.16) | async-done | bytes 1064992 | tf_op jit(solution)/shard_map/all_to_all | solution.py:378
  78.4 4.1 %all-to-all-start.17 = ((f32[32,65,1,128]{3,2,1,0:T(1,128)}), f32[32,65,1,128]{3,2,1,0:T(1,128)S(1)}, u32[]{:S(2)}, u32[]{:S(2)}) async-start(f32[32,65,1,128]{3,2,1,0:T(1,128)} %bitcast.32), calls=%async_computation.17 | async-start | bytes 2129920 | tf_op jit(solution)/shard_map/all_to_all | solution.py:378
  82.5 3.8 %repack.2 = (f32[320,128]{1,0:T(8,128)S(1)}, f32[320,128]{1,0:T(8,128)S(1)}, f32[320,128]{1,0:T(8,128)S(1)}, f32[320,128]{1,0:T(8,128)S(1)}, f32[384,128]{1,0:T(...) custom-call(s32[1]{0:T(128)} %bitcast.27.me_ref, f32[2080,128]{1,0:T(8,128)S(1)} %bitcast.149), custom_call_target="tpu_custom_call" | custom-call | tf_op jit(solution)/shard_map/repack/pallas_call | solution.py:198
  86.3 3.1 %collective-permute-start = (f32[320,128]{1,0:T(8,128)S(1)}, f32[320,128]{1,0:T(8,128)S(1)}, u32[]{:S(2)}, u32[]{:S(2)}) collective-permute-start(f32[320,128]{1,0:T(8,128)S(1)} %get-tuple-element.56), channel_id=1, source_target_pairs={{0,32},{32,64},{64,96},{96,0},{128,160},{160,192},{192,224},{224,1... | collective-permute-start | bytes 491528 | tf_op jit(solution)/shard_map/ppermute | solution.py:344
  89.4 4.4 %collective-permute-start.1 = (f32[320,128]{1,0:T(8,128)S(1)}, f32[320,128]{1,0:T(8,128)S(1)}, u32[]{:S(2)}, u32[]{:S(2)}) collective-permute-start(f32[320,128]{1,0:T(8,128)S(1)} %get-tuple-element.57), channel_id=1, source_target_pairs={{0,64},{32,96},{64,0},{96,32},{128,192},{160,224},{192,128},{224,1... | collective-permute-start | bytes 491528 | tf_op jit(solution)/shard_map/ppermute | solution.py:344
  93.8 3.1 %collective-permute-start.2 = (f32[320,128]{1,0:T(8,128)S(1)}, f32[320,128]{1,0:T(8,128)S(1)}, u32[]{:S(2)}, u32[]{:S(2)}) collective-permute-start(f32[320,128]{1,0:T(8,128)S(1)} %get-tuple-element.58), channel_id=1, source_target_pairs={{0,96},{32,0},{64,32},{96,64},{128,224},{160,128},{192,160},{224,1... | collective-permute-start | bytes 491528 | tf_op jit(solution)/shard_map/ppermute | solution.py:344
  96.9 3.2 %collective-permute-start.6 = (f32[384,128]{1,0:T(8,128)S(1)}, f32[384,128]{1,0:T(8,128)S(1)}, u32[]{:S(2)}, u32[]{:S(2)}) collective-permute-start(f32[384,128]{1,0:T(8,128)S(1)} %get-tuple-element.60), channel_id=1, source_target_pairs={{0,128},{32,160},{64,192},{96,224},{128,256},{160,288},{192,320},{... | collective-permute-start | bytes 589832 | tf_op jit(solution)/shard_map/ppermute | solution.py:344
  100.1 4.5 %collective-permute-start.7 = (f32[384,128]{1,0:T(8,128)S(1)}, f32[384,128]{1,0:T(8,128)S(1)}, u32[]{:S(2)}, u32[]{:S(2)}) collective-permute-start(f32[384,128]{1,0:T(8,128)S(1)} %get-tuple-element.61), channel_id=1, source_target_pairs={{0,256},{32,288},{64,320},{96,352},{128,384},{160,416},{192,448},{... | collective-permute-start | bytes 589832 | tf_op jit(solution)/shard_map/ppermute | solution.py:344
  104.7 3.0 %collective-permute-start.8 = (f32[384,128]{1,0:T(8,128)S(1)}, f32[384,128]{1,0:T(8,128)S(1)}, u32[]{:S(2)}, u32[]{:S(2)}) collective-permute-start(f32[384,128]{1,0:T(8,128)S(1)} %get-tuple-element.62), channel_id=1, source_target_pairs={{0,384},{32,416},{64,448},{96,480},{128,0},{160,32},{192,64},{224,... | collective-permute-start | bytes 589832 | tf_op jit(solution)/shard_map/ppermute | solution.py:344
  110.1 2.7 %collective-permute-start.4 = (f32[320,128]{1,0:T(8,128)S(1)}, f32[320,128]{1,0:T(8,128)S(1)}, u32[]{:S(2)}, u32[]{:S(2)}) collective-permute-start(f32[320,128]{1,0:T(8,128)S(1)} %pad_maximum_fusion.6), channel_id=1, source_target_pairs={{0,256},{32,288},{64,320},{96,352},{128,384},{160,416},{192,448},{... | collective-permute-start | bytes 491528 | tf_op jit(solution)/shard_map/ppermute | solution.py:344
  115.2 2.8 %collective-permute-start.10 = (f32[384,128]{1,0:T(8,128)S(1)}, f32[384,128]{1,0:T(8,128)S(1)}, u32[]{:S(2)}, u32[]{:S(2)}) collective-permute-start(f32[384,128]{1,0:T(8,128)S(1)} %pad_maximum_fusion.3), channel_id=1, source_target_pairs={{0,64},{32,96},{64,0},{96,32},{128,192},{160,224},{192,128},{224,1... | collective-permute-start | bytes 589832 | tf_op jit(solution)/shard_map/ppermute | solution.py:344
  118.0 3.4 %collective-permute-start.11 = (f32[384,128]{1,0:T(8,128)S(1)}, f32[384,128]{1,0:T(8,128)S(1)}, u32[]{:S(2)}, u32[]{:S(2)}) collective-permute-start(f32[384,128]{1,0:T(8,128)S(1)} %pad_maximum_fusion.4), channel_id=1, source_target_pairs={{0,96},{32,0},{64,32},{96,64},{128,224},{160,128},{192,160},{224,1... | collective-permute-start | bytes 589832 | tf_op jit(solution)/shard_map/ppermute | solution.py:344
  122.1 3.5 %collective-permute-start.5 = (f32[320,128]{1,0:T(8,128)S(1)}, f32[320,128]{1,0:T(8,128)S(1)}, u32[]{:S(2)}, u32[]{:S(2)}) collective-permute-start(f32[320,128]{1,0:T(8,128)S(1)} %pad_maximum_fusion.7), channel_id=1, source_target_pairs={{0,384},{32,416},{64,448},{96,480},{128,0},{160,32},{192,64},{224,... | collective-permute-start | bytes 491528 | tf_op jit(solution)/shard_map/ppermute | solution.py:344
  126.3 3.1 %collective-permute-done.5.refs_6_ = f32[320,128]{1,0:T(8,128)S(1)} collective-permute-done((f32[320,128]{1,0:T(8,128)S(1)}, f32[320,128]{1,0:T(8,128)S(1)}, u32[]{:S(2)}, u32[]{:S(2)}) %collective-permute-start.5) | collective-permute-done | bytes 163872 | tf_op jit(solution)/shard_map/ppermute | solution.py:344
  130.1 8.9 %all-to-all-done.17 = f32[32,65,1,128]{3,2,1,0:T(1,128)S(1)} async-done(((f32[32,65,1,128]{3,2,1,0:T(1,128)}), f32[32,65,1,128]{3,2,1,0:T(1,128)S(1)}, u32[]{:S(2)}, u32[]{:S(2)}) %all-to-all-start.17) | async-done | bytes 1064992 | tf_op jit(solution)/shard_map/all_to_all | solution.py:378
  139.0 4.9 %repack.3 = f32[2816,128]{1,0:T(8,128)} custom-call(s32[1]{0:T(128)} %bitcast.27.me_ref, f32[2080,128]{1,0:T(8,128)S(1)} %bitcast.147), custom_call_target="tpu_custom_call" | custom-call | tf_op jit(solution)/shard_map/repack/pallas_call | solution.py:198
  143.9 6.9 %all-to-all-start.18 = ((f32[16,176,128]{2,1,0:T(8,128)}), f32[16,176,128]{2,1,0:T(8,128)S(1)}, u32[]{:S(2)}, u32[]{:S(2)}) async-start(f32[16,176,128]{2,1,0:T(8,128)} %bitcast.34), calls=%async_computation.18 | async-start | bytes 2883584 | tf_op jit(solution)/shard_map/all_to_all | solution.py:390
  154.3 5.1 %solve.2 = (f32[64,128]{1,0:T(8,128)S(1)}, f32[1,128]{1,0:T(1,128)S(1)}) custom-call(f32[64,128]{1,0:T(8,128)S(1)} %constant_dynamic-slice_fusion.cur_ref, f32[1,128]{1,0:T(1,128)S(1)} %bitcast.159, f32[1,128]{1,0:T(1,128)S(1)} %broadcast_in_dim.29.seen_ref, f32[320,128]{1,0:T(8,128)S(1)} %get-tuple-element.64.refs_0_, ...), custom_call_target="tpu_custom_call" | custom-call | tf_op jit(solution)/shard_map/solve/pallas_call | solution.py:273
  159.4 11.2 %all-to-all-done.18 = f32[16,176,128]{2,1,0:T(8,128)S(1)} async-done(((f32[16,176,128]{2,1,0:T(8,128)}), f32[16,176,128]{2,1,0:T(8,128)S(1)}, u32[]{:S(2)}, u32[]{:S(2)}) %all-to-all-start.18) | async-done | bytes 1441824 | tf_op jit(solution)/shard_map/all_to_all | solution.py:390
  170.6 5.0 %solve.3 = (f32[64,128]{1,0:T(8,128)S(1)}, f32[1,128]{1,0:T(1,128)S(1)}) custom-call(f32[64,128]{1,0:T(8,128)S(1)} %get-tuple-element.78.cur_ref, f32[1,128]{1,0:T(1,128)S(1)} %bitcast.160, f32[1,128]{1,0:T(1,128)S(1)} %get-tuple-element.79.seen_ref, f32[2816,128]{1,0:T(8,128)S(1)} %bitcast.143), custom_call_target="tpu_custom_call" | custom-call | tf_op jit(solution)/shard_map/solve/pallas_call | solution.py:273
  176.0 16.3 %all_to_all.91 = f32[16,64,128]{2,1,0:T(8,128)S(1)} all-to-all(f32[16,64,128]{2,1,0:T(8,128)S(1)} %broadcast_in_dim.30), channel_id=1, replica_groups=mesh['dp'=16,'cent'=32] {'dp'}, dimensions={0} | all-to-all | bytes 1048576 | tf_op jit(solution)/shard_map/all_to_all | solution.py:401
  (61 shorter events, 13.9 us)
Async XLA Ops:
  0.8 1.0 copy-start
  5.1 16.9 %copy-start.1 = (f32[1024,128]{1,0:T(8,128)S(1)}, f32[1024,128]{1,0:T(8,128)}, u32[]{:S(2)}) copy-start(f32[1024,128]{1,0:T(8,128)} %x_ref.3) | copy-start | bytes 1572868
  5.1 16.9 %copy-start.9 = (f32[1024]{0:T(1024)S(1)}, f32[1024]{0:T(1024)}, u32[]{:S(2)}) copy-start(f32[1024]{0:T(1024)} %param.10) | copy-start | bytes 12292
  5.1 73.3 %all-to-all-start.16 = ((f32[32,65,1,128]{3,2,1,0:T(1,128)}), f32[32,65,1,128]{3,2,1,0:T(1,128)S(1)}, u32[]{:S(2)}, u32[]{:S(2)}) async-start(f32[32,65,1,128]{3,2,1,0:T(1,128)} %bitcast.30), calls=%async_computation.16 | async-start | bytes 2129920 | tf_op jit(solution)/shard_map/all_to_all | solution.py:378
  78.4 7.9 %copy-start.14 = (f32[32,65,1,128]{3,2,1,0:T(1,128)}, f32[32,65,1,128]{3,2,1,0:T(1,128)S(1)}, u32[]{:S(2)}) copy-start(f32[32,65,1,128]{3,2,1,0:T(1,128)S(1)} %all-to-all-done.16) | copy-start | bytes 3194884
  78.4 60.6 %all-to-all-start.17 = ((f32[32,65,1,128]{3,2,1,0:T(1,128)}), f32[32,65,1,128]{3,2,1,0:T(1,128)S(1)}, u32[]{:S(2)}, u32[]{:S(2)}) async-start(f32[32,65,1,128]{3,2,1,0:T(1,128)} %bitcast.32), calls=%async_computation.17 | async-start | bytes 2129920 | tf_op jit(solution)/shard_map/all_to_all | solution.py:378
  86.3 18.4 %collective-permute-start = (f32[320,128]{1,0:T(8,128)S(1)}, f32[320,128]{1,0:T(8,128)S(1)}, u32[]{:S(2)}, u32[]{:S(2)}) collective-permute-start(f32[320,128]{1,0:T(8,128)S(1)} %get-tuple-element.56), channel_id=1, source_target_pairs={{0,32},{32,64},{64,96},{96,0},{128,160},{160,192},{192,224},{224,1... | collective-permute-start | bytes 491528 | tf_op jit(solution)/shard_map/ppermute | solution.py:344
  89.4 18.2 %collective-permute-start.1 = (f32[320,128]{1,0:T(8,128)S(1)}, f32[320,128]{1,0:T(8,128)S(1)}, u32[]{:S(2)}, u32[]{:S(2)}) collective-permute-start(f32[320,128]{1,0:T(8,128)S(1)} %get-tuple-element.57), channel_id=1, source_target_pairs={{0,64},{32,96},{64,0},{96,32},{128,192},{160,224},{192,128},{224,1... | collective-permute-start | bytes 491528 | tf_op jit(solution)/shard_map/ppermute | solution.py:344
  93.8 13.9 %collective-permute-start.2 = (f32[320,128]{1,0:T(8,128)S(1)}, f32[320,128]{1,0:T(8,128)S(1)}, u32[]{:S(2)}, u32[]{:S(2)}) collective-permute-start(f32[320,128]{1,0:T(8,128)S(1)} %get-tuple-element.58), channel_id=1, source_target_pairs={{0,96},{32,0},{64,32},{96,64},{128,224},{160,128},{192,160},{224,1... | collective-permute-start | bytes 491528 | tf_op jit(solution)/shard_map/ppermute | solution.py:344
  96.9 15.9 %collective-permute-start.6 = (f32[384,128]{1,0:T(8,128)S(1)}, f32[384,128]{1,0:T(8,128)S(1)}, u32[]{:S(2)}, u32[]{:S(2)}) collective-permute-start(f32[384,128]{1,0:T(8,128)S(1)} %get-tuple-element.60), channel_id=1, source_target_pairs={{0,128},{32,160},{64,192},{96,224},{128,256},{160,288},{192,320},{... | collective-permute-start | bytes 589832 | tf_op jit(solution)/shard_map/ppermute | solution.py:344
  100.1 12.8 %collective-permute-start.7 = (f32[384,128]{1,0:T(8,128)S(1)}, f32[384,128]{1,0:T(8,128)S(1)}, u32[]{:S(2)}, u32[]{:S(2)}) collective-permute-start(f32[384,128]{1,0:T(8,128)S(1)} %get-tuple-element.61), channel_id=1, source_target_pairs={{0,256},{32,288},{64,320},{96,352},{128,384},{160,416},{192,448},{... | collective-permute-start | bytes 589832 | tf_op jit(solution)/shard_map/ppermute | solution.py:344
  104.7 8.2 %collective-permute-start.8 = (f32[384,128]{1,0:T(8,128)S(1)}, f32[384,128]{1,0:T(8,128)S(1)}, u32[]{:S(2)}, u32[]{:S(2)}) collective-permute-start(f32[384,128]{1,0:T(8,128)S(1)} %get-tuple-element.62), channel_id=1, source_target_pairs={{0,384},{32,416},{64,448},{96,480},{128,0},{160,32},{192,64},{224,... | collective-permute-start | bytes 589832 | tf_op jit(solution)/shard_map/ppermute | solution.py:344
  107.8 13.7 %collective-permute-start.3 = (f32[320,128]{1,0:T(8,128)S(1)}, f32[320,128]{1,0:T(8,128)S(1)}, u32[]{:S(2)}, u32[]{:S(2)}) collective-permute-start(f32[320,128]{1,0:T(8,128)S(1)} %pad_maximum_fusion.5), channel_id=1, source_target_pairs={{0,128},{32,160},{64,192},{96,224},{128,256},{160,288},{192,320},{... | collective-permute-start | bytes 491528 | tf_op jit(solution)/shard_map/ppermute | solution.py:344
  110.1 15.6 %collective-permute-start.4 = (f32[320,128]{1,0:T(8,128)S(1)}, f32[320,128]{1,0:T(8,128)S(1)}, u32[]{:S(2)}, u32[]{:S(2)}) collective-permute-start(f32[320,128]{1,0:T(8,128)S(1)} %pad_maximum_fusion.6), channel_id=1, source_target_pairs={{0,256},{32,288},{64,320},{96,352},{128,384},{160,416},{192,448},{... | collective-permute-start | bytes 491528 | tf_op jit(solution)/shard_map/ppermute | solution.py:344
  112.9 17.2 %collective-permute-start.9 = (f32[384,128]{1,0:T(8,128)S(1)}, f32[384,128]{1,0:T(8,128)S(1)}, u32[]{:S(2)}, u32[]{:S(2)}) collective-permute-start(f32[384,128]{1,0:T(8,128)S(1)} %pad_maximum_fusion.2), channel_id=1, source_target_pairs={{0,32},{32,64},{64,96},{96,0},{128,160},{160,192},{192,224},{224,1... | collective-permute-start | bytes 589832 | tf_op jit(solution)/shard_map/ppermute | solution.py:344
  115.2 14.9 %collective-permute-start.10 = (f32[384,128]{1,0:T(8,128)S(1)}, f32[384,128]{1,0:T(8,128)S(1)}, u32[]{:S(2)}, u32[]{:S(2)}) collective-permute-start(f32[384,128]{1,0:T(8,128)S(1)} %pad_maximum_fusion.3), channel_id=1, source_target_pairs={{0,64},{32,96},{64,0},{96,32},{128,192},{160,224},{192,128},{224,1... | collective-permute-start | bytes 589832 | tf_op jit(solution)/shard_map/ppermute | solution.py:344
  118.0 12.1 %collective-permute-start.11 = (f32[384,128]{1,0:T(8,128)S(1)}, f32[384,128]{1,0:T(8,128)S(1)}, u32[]{:S(2)}, u32[]{:S(2)}) collective-permute-start(f32[384,128]{1,0:T(8,128)S(1)} %pad_maximum_fusion.4), channel_id=1, source_target_pairs={{0,96},{32,0},{64,32},{96,64},{128,224},{160,128},{192,160},{224,1... | collective-permute-start | bytes 589832 | tf_op jit(solution)/shard_map/ppermute | solution.py:344
  122.1 7.3 %collective-permute-start.5 = (f32[320,128]{1,0:T(8,128)S(1)}, f32[320,128]{1,0:T(8,128)S(1)}, u32[]{:S(2)}, u32[]{:S(2)}) collective-permute-start(f32[320,128]{1,0:T(8,128)S(1)} %pad_maximum_fusion.7), channel_id=1, source_target_pairs={{0,384},{32,416},{64,448},{96,480},{128,0},{160,32},{192,64},{224,... | collective-permute-start | bytes 491528 | tf_op jit(solution)/shard_map/ppermute | solution.py:344
  139.0 4.9 %copy-start.12 = (f32[32,65,1,128]{3,2,1,0:T(1,128)}, f32[32,65,1,128]{3,2,1,0:T(1,128)S(1)}, u32[]{:S(2)}) copy-start(f32[32,65,1,128]{3,2,1,0:T(1,128)S(1)} %all-to-all-done.17) | copy-start | bytes 3194884
  143.9 7.7 %copy-start.26 = (f32[128]{0:T(128)S(1)}, f32[128]{0:T(128)}, u32[]{:S(2)}) copy-start(f32[128]{0:T(128)} %param.13) | copy-start | bytes 1540
  143.9 26.7 %all-to-all-start.18 = ((f32[16,176,128]{2,1,0:T(8,128)}), f32[16,176,128]{2,1,0:T(8,128)S(1)}, u32[]{:S(2)}, u32[]{:S(2)}) async-start(f32[16,176,128]{2,1,0:T(8,128)} %bitcast.34), calls=%async_computation.18 | async-start | bytes 2883584 | tf_op jit(solution)/shard_map/all_to_all | solution.py:390
  151.6 0.9 copy-start.3
  153.4 0.9 copy-start.7
  159.4 16.3 %copy-start.15 = (f32[32,65,1,128]{3,2,1,0:T(1,128)S(1)}, f32[32,65,1,128]{3,2,1,0:T(1,128)}, u32[]{:S(2)}) copy-start(f32[32,65,1,128]{3,2,1,0:T(1,128)} %copy-done.14) | copy-start | bytes 3194884
  (5 other events, 3.6 us)
